TPU v7x, 256 devices: a whole 4x4x8 slice. The times are simulated.
256 devices in a mesh: gx: 32 (over z, y), col: 8 (over x, core).
Axes of the slice: x: 4, y: 4, z: 8, core: 2. Of those that a mesh axis runs over, the one named last changes fastest.
Arguments:
- propagator: float32 [8, 64, 512, 256], P('col', None, 'gx'), may hold values from -4 to 4
- complement: bfloat16 [8, 2, 64, 512, 256], P('col', None, None, 'gx'), may hold values from -0.75 to 0.75
- labels: int32 [8, 2], P('col'), may hold values from 0 to 1
- absorption: float32 [2, 512, 256], P(None, 'gx'), may hold values from 0 to 2048
- to_ordinates: float32 [64, 64], replicated, may hold values from -0.75 to 0.75
- to_modes: float32 [64, 64], replicated, may hold values from -0.75 to 0.75
- upwind: float32 [64], replicated, may hold values from 32 to 4096
- mode_decay: float32 [2, 64], replicated, may hold values from 0.3 to 1
Outputs:
- propagated: float32 [8, 64, 512, 256], P('col', None, 'gx')
- segment_density: float32 [2, 512, 256], P(None, 'gx')
All inputs are finite; a program needn't handle non-finite values.
Results may differ from a plain program's by a relative error of at most 0.0003.
Values sent between devices are 32-bit elements; how exact they have to be, the bound alone decides.
A program may use at most 64 MiB of HBM per device.

v0:
```python
import jax
import jax.numpy as jnp
from jax import lax
from jax.sharding import PartitionSpec as P


def carried_in(value, axis, join, neutral, backward):
    count, mine = (lax.axis_size(axis), lax.axis_index(axis))
    pieces = jax.tree.map(lambda part: lax.all_gather(part, axis), value)
    if backward:
        pieces = jax.tree.map(lambda part: part[::-1], pieces)
        mine = count - 1 - mine
    subtotal = jax.tree.map(
        lambda part, zero: jnp.full_like(part, 0) + jnp.asarray(zero, part.dtype), value, neutral
    )

    def step(position, subtotal):
        longer = join(subtotal, jax.tree.map(lambda part: part[position], pieces))
        return jax.tree.map(lambda new, old: jnp.where(position < mine, new, old), longer, subtotal)

    return lax.fori_loop(0, count - 1, step, subtotal)


def spread(x, axis, root):
    mine = lax.axis_index(axis) == root
    return lax.psum(jnp.where(mine, x, jnp.zeros_like(x)), axis)


def compose_maps(first_map, second_map):
    return (first_map[0] * second_map[0], second_map[0] * first_map[1] + second_map[1])


def local_sweep(ordinal, coeffs, absorb_now, reverse):

    def advance(state, item):
        source, absorb_row = item
        free_part, unit_part = state
        denominator = 1.0 + coeffs + absorb_row[None, :]
        free_part = (source + coeffs * free_part) / denominator
        unit_part = coeffs * unit_part / denominator
        return ((free_part, unit_part), (free_part, unit_part))

    initial = (jnp.zeros(ordinal.shape[1:], jnp.float32), jnp.ones(ordinal.shape[1:], jnp.float32))
    _, (free_all, unit_all) = lax.scan(advance, initial, (ordinal, absorb_now), reverse=reverse)
    return (free_all, unit_all)


def body(propagator, complement, labels, absorption, to_ordinates, to_modes, upwind, mode_decay):
    half_modes = upwind.shape[0] // 2
    coeff_fwd = upwind[:half_modes][:, None]
    coeff_bwd = upwind[half_modes:][:, None]
    section = propagator[0]
    density = jnp.zeros(absorption.shape, jnp.float32)
    cycle_size = lax.axis_size("gx")
    for contour_step in range(complement.shape[1]):
        first_species = labels[0, contour_step] == 0
        absorb_now = jnp.where(first_species, absorption[0], absorption[1])
        mode_gain = jnp.where(first_species, mode_decay[0], mode_decay[1])
        ordinal = jnp.einsum("nm,mxl->xnl", to_ordinates, section, precision=lax.Precision.HIGHEST)
        free_fwd, unit_fwd = local_sweep(ordinal[:, :half_modes], coeff_fwd, absorb_now, False)
        free_bwd, unit_bwd = local_sweep(ordinal[:, half_modes:], coeff_bwd, absorb_now, True)
        fwd_map = (unit_fwd[-1], free_fwd[-1])
        bwd_map = (unit_bwd[0], free_bwd[0])
        identity_map = (jnp.ones_like(fwd_map[0]), jnp.zeros_like(fwd_map[1]))
        prefix_fwd = carried_in(fwd_map, "gx", compose_maps, identity_map, False)
        whole_fwd = compose_maps(prefix_fwd, fwd_map)
        closing_fwd = spread(jnp.stack(whole_fwd), "gx", cycle_size - 1)
        entry_fwd = closing_fwd[1] / (1.0 - closing_fwd[0])
        inflow_fwd = prefix_fwd[0] * entry_fwd + prefix_fwd[1]
        prefix_bwd = carried_in(bwd_map, "gx", compose_maps, identity_map, True)
        whole_bwd = compose_maps(prefix_bwd, bwd_map)
        closing_bwd = spread(jnp.stack(whole_bwd), "gx", 0)
        entry_bwd = closing_bwd[1] / (1.0 - closing_bwd[0])
        inflow_bwd = prefix_bwd[0] * entry_bwd + prefix_bwd[1]
        solved_fwd = free_fwd + unit_fwd * inflow_fwd[None]
        solved_bwd = free_bwd + unit_bwd * inflow_bwd[None]
        solved_ord = jnp.concatenate([solved_fwd, solved_bwd], axis=1)
        section = mode_gain[:, None, None] * jnp.einsum(
            "mn,xnl->mxl", to_modes, solved_ord, precision=lax.Precision.HIGHEST
        )
        density_term = jnp.sum(section * complement[0, contour_step].astype(jnp.float32), axis=0)
        step_density = jnp.stack(
            [
                jnp.where(first_species, density_term, 0.0),
                jnp.where(first_species, 0.0, density_term),
            ]
        )
        density = density + step_density
    density = lax.psum(density, "col")
    return (section[None], density)


def solution(mesh):
    in_specs = (
        P("col", None, "gx", None),
        P("col", None, None, "gx", None),
        P("col", None),
        P(None, "gx", None),
        P(),
        P(),
        P(),
        P(),
    )
    out_specs = (P("col", None, "gx", None), P(None, "gx", None))
    return jax.shard_map(body, mesh=mesh, in_specs=in_specs, out_specs=out_specs, check_vma=False)
```

profile of v0, /device:TPU:1, one launch (start us, length us, event | category | flops | bytes accessed | tf_op | source)
XLA Modules:
  0.0 1007.8 jit_solution(349088183387521213)
XLA Ops:
  9.9 2.9 convolution_bitcast_fusion.1
  13.6 2.3 while.140
  17.5 2.3 while.142
  21.3 1.3 fusion.46
  22.6 69.8 %all-gather.11.cloned.1.call-done = f32[32,32,256]{2,1,0:T(8,128)} async-done(((f32[1,32,256]{2,1,0:T(8,128)}), f32[32,32,256]{2,1,0:T(8,128)}) %all-gather.11.cloned.1.call-update) | async-done | bytes 1048592 | tf_op jit(solution)/shard_map/all_gather | solution.py:9
  92.3 77.0 %all-gather.9.cloned.1.call-done = f32[32,32,256]{2,1,0:T(8,128)} async-done(((f32[1,32,256]{2,1,0:T(8,128)}), f32[32,32,256]{2,1,0:T(8,128)}) %all-gather.9.cloned.1.call-update) | async-done | bytes 1048592 | tf_op jit(solution)/shard_map/all_gather | solution.py:9
  169.4 25.4 %while.141 = (s32[]{:T(128)}, f32[32,256]{1,0:T(8,128)S(1)}, f32[32,256]{1,0:T(8,128)S(1)}, s32[]{:T(128)}, f32[32,32,256]{2,1,0:T(8,128)}, /*index=5*/f32[32,32,256]{2,1,0:T(8,128)}, s32[]{:T(128)}, s32[]{:T(128)}) while((s32[]{:T(128)}, f32[32,256]{1,0:T(8,128)S(1)}, f32[32,256]{1,0:T(8,128)S(1)}, s32[]{:T(128)}, ...), condition=%wide.region_3.4_spmd.clone, body=%wide.region_2.3_spmd.clone.sunk | while | flops 57348 | bytes 196717 | solution.py:21
  170.2 0.8 fusion.55
  171.0 0.8 fusion.55
  171.8 0.8 fusion.55
  172.6 0.8 fusion.55
  173.5 0.8 fusion.55
  174.3 0.8 fusion.55
  175.1 0.8 fusion.55
  175.9 0.8 fusion.55
  176.7 0.8 fusion.55
  177.6 0.8 fusion.55
  178.4 0.8 fusion.55
  181.7 0.8 fusion.55
  182.5 0.8 fusion.55
  183.3 0.8 fusion.55
  185.7 0.8 fusion.55
  186.6 0.8 fusion.55
  187.4 0.8 fusion.55
  192.3 0.8 fusion.55
  194.7 51.7 %all-gather.13.cloned.1.call-done = f32[32,32,256]{2,1,0:T(8,128)} async-done(((f32[1,32,256]{2,1,0:T(8,128)}), f32[32,32,256]{2,1,0:T(8,128)}) %all-gather.13.cloned.1.call-update) | async-done | bytes 1048592 | tf_op jit(solution)/shard_map/all_gather | solution.py:9
  246.4 2.3 rev.12
  248.7 74.0 %all-gather.15.cloned.1.call-done = f32[32,32,256]{2,1,0:T(8,128)} async-done(((f32[1,32,256]{2,1,0:T(8,128)}), f32[32,32,256]{2,1,0:T(8,128)}) %all-gather.15.cloned.1.call-update) | async-done | bytes 1048592 | tf_op jit(solution)/shard_map/all_gather | solution.py:9
  322.7 2.3 rev.13
  325.0 25.4 %while.143 = (s32[]{:T(128)}, f32[32,256]{1,0:T(8,128)S(1)}, f32[32,256]{1,0:T(8,128)S(1)}, s32[]{:T(128)}, f32[32,32,256]{2,1,0:T(8,128)}, /*index=5*/f32[32,32,256]{2,1,0:T(8,128)}, s32[]{:T(128)}, s32[]{:T(128)}) while((s32[]{:T(128)}, f32[32,256]{1,0:T(8,128)S(1)}, f32[32,256]{1,0:T(8,128)S(1)}, s32[]{:T(128)}, ...), condition=%wide.region_8.9_spmd.clone, body=%wide.region_7.8_spmd.clone.sunk | while | flops 57348 | bytes 196717 | solution.py:21
  327.5 0.8 fusion.56
  329.9 0.8 fusion.56
  336.5 0.8 fusion.56
  343.1 0.8 fusion.56
  345.5 0.8 fusion.56
  352.4 138.0 %all-reduce.7.cloned.1.call-done = (f32[2,32,256]{2,1,0:T(8,128)}, f32[2,32,256]{2,1,0:T(8,128)}) async-done(((f32[2,32,256]{2,1,0:T(8,128)}, f32[2,32,256]{2,1,0:T(8,128)}), (f32[2,32,256]{2,1,0:T(8,128)}, f32[2,32,256]{2,1,0:T(8,128)})) %all-reduce.7.cloned.1.call-update) | async-done | bytes 131088 | tf_op jit(solution)/shard_map/psum | solution.py:26
  490.4 0.8 fusion.25
  491.4 1.3 fusion.12
  492.7 1.1 convolution_bitcast_fusion
  494.0 2.3 while.144
  497.8 2.3 while.146
  501.6 70.3 %all-gather.17.cloned.1.call-done = f32[32,32,256]{2,1,0:T(8,128)} async-done(((f32[1,32,256]{2,1,0:T(8,128)}), f32[32,32,256]{2,1,0:T(8,128)}) %all-gather.17.cloned.1.call-update) | async-done | bytes 1048592 | tf_op jit(solution)/shard_map/all_gather | solution.py:9
  571.8 76.8 %all-gather.19.cloned.1.call-done = f32[32,32,256]{2,1,0:T(8,128)} async-done(((f32[1,32,256]{2,1,0:T(8,128)}), f32[32,32,256]{2,1,0:T(8,128)}) %all-gather.19.cloned.1.call-update) | async-done | bytes 1048592 | tf_op jit(solution)/shard_map/all_gather | solution.py:9
  648.6 25.3 %while.145 = (s32[]{:T(128)}, f32[32,256]{1,0:T(8,128)S(1)}, f32[32,256]{1,0:T(8,128)S(1)}, s32[]{:T(128)}, f32[32,32,256]{2,1,0:T(8,128)}, /*index=5*/f32[32,32,256]{2,1,0:T(8,128)}, s32[]{:T(128)}, s32[]{:T(128)}) while((s32[]{:T(128)}, f32[32,256]{1,0:T(8,128)S(1)}, f32[32,256]{1,0:T(8,128)S(1)}, s32[]{:T(128)}, ...), condition=%wide.region_13.14_spmd.clone, body=%wide.region_12.13_spmd.clone.sunk | while | flops 57348 | bytes 196717 | solution.py:21
  660.1 0.8 fusion.57
  660.9 0.8 fusion.57
  661.7 0.8 fusion.57
  665.8 0.8 fusion.57
  666.6 0.8 fusion.57
  667.5 0.8 fusion.57
  674.0 52.0 %all-gather.21.cloned.1.call-done = f32[32,32,256]{2,1,0:T(8,128)} async-done(((f32[1,32,256]{2,1,0:T(8,128)}), f32[32,32,256]{2,1,0:T(8,128)}) %all-gather.21.cloned.1.call-update) | async-done | bytes 1048592 | tf_op jit(solution)/shard_map/all_gather | solution.py:9
  726.0 2.3 rev.14
  728.3 74.5 %all-gather.23.cloned.1.call-done = f32[32,32,256]{2,1,0:T(8,128)} async-done(((f32[1,32,256]{2,1,0:T(8,128)}), f32[32,32,256]{2,1,0:T(8,128)}) %all-gather.23.cloned.1.call-update) | async-done | bytes 1048592 | tf_op jit(solution)/shard_map/all_gather | solution.py:9
  802.8 2.4 rev.15
  805.2 25.4 %while.147 = (s32[]{:T(128)}, f32[32,256]{1,0:T(8,128)S(1)}, f32[32,256]{1,0:T(8,128)S(1)}, s32[]{:T(128)}, f32[32,32,256]{2,1,0:T(8,128)}, /*index=5*/f32[32,32,256]{2,1,0:T(8,128)}, s32[]{:T(128)}, s32[]{:T(128)}) while((s32[]{:T(128)}, f32[32,256]{1,0:T(8,128)S(1)}, f32[32,256]{1,0:T(8,128)S(1)}, s32[]{:T(128)}, ...), condition=%wide.region_18.19_spmd.clone, body=%wide.region_17.18_spmd.clone.sunk | while | flops 57348 | bytes 196717 | solution.py:21
  809.2 0.8 fusion.58
  811.7 0.8 fusion.58
  818.3 0.8 fusion.58
  824.8 0.8 fusion.58
  827.3 0.8 fusion.58
  831.9 138.7 %all-reduce.5.cloned.1.call-done = (f32[2,32,256]{2,1,0:T(8,128)}, f32[2,32,256]{2,1,0:T(8,128)}) async-done(((f32[2,32,256]{2,1,0:T(8,128)}, f32[2,32,256]{2,1,0:T(8,128)}), (f32[2,32,256]{2,1,0:T(8,128)}, f32[2,32,256]{2,1,0:T(8,128)})) %all-reduce.5.cloned.1.call-update) | async-done | bytes 131088 | tf_op jit(solution)/shard_map/psum | solution.py:26
  972.3 1.3 fusion.11
  973.6 25.8 %psum.39 = f32[2,16,256]{2,1,0:T(8,128)} all-reduce(f32[2,16,256]{2,1,0:T(8,128)S(1)} %maximum_add_fusion), channel_id=1, replica_groups=mesh['gx'=32,'col'=8] {'col'}, use_global_device_ids=true, to_apply=%region_22.23 | all-reduce | flops 8192 | bytes 65536 | tf_op jit(solution)/shard_map/psum | solution.py:89
  999.3 1.6 copy.17
  (371 shorter events, 91.5 us)
Async XLA Ops:
  7.2 484.3 %copy-start = (f32[64,64]{1,0:T(8,128)S(1)}, f32[64,64]{1,0:T(8,128)}, u32[]{:S(2)}) copy-start(f32[64,64]{1,0:T(8,128)} %param.29) | copy-start | bytes 49156
  7.2 85.2 %all-gather.11.cloned.1.call-start = ((), (), s32[]{:S(2)}) async-start(), calls=%async_computation.1 | async-start | bytes 1081344 | tf_op jit(solution)/shard_map/all_gather | solution.py:9
  7.2 0.7 copy-start.4
  9.1 0.7 copy-start.5
  12.8 0.8 copy-start.3
  16.6 152.8 %all-gather.9.cloned.1.call-start = ((), (), s32[]{:S(2)}) async-start(), calls=%async_computation | async-start | bytes 1081344 | tf_op jit(solution)/shard_map/all_gather | solution.py:9
  17.3 229.1 %all-gather.13.cloned.1.call-start = ((), (), s32[]{:S(2)}) async-start(), calls=%async_computation.2 | async-start | bytes 1081344 | tf_op jit(solution)/shard_map/all_gather | solution.py:9
  20.5 302.3 %all-gather.15.cloned.1.call-start = ((), (), s32[]{:S(2)}) async-start(), calls=%async_computation.3 | async-start | bytes 1081344 | tf_op jit(solution)/shard_map/all_gather | solution.py:9
  21.2 469.3 %all-reduce.7.cloned.1.call-start = ((), (), s32[]{:S(2)}) async-start(), calls=%async_computation.9 | async-start | bytes 262144 | tf_op jit(solution)/shard_map/psum | solution.py:26
  351.7 0.7 copy-start.6
  351.7 220.1 %all-gather.17.cloned.1.call-start = ((), (), s32[]{:S(2)}) async-start(), calls=%async_computation.4 | async-start | bytes 1081344 | tf_op jit(solution)/shard_map/all_gather | solution.py:9
  491.4 1.3 copy-start.1
  496.9 151.7 %all-gather.19.cloned.1.call-start = ((), (), s32[]{:S(2)}) async-start(), calls=%async_computation.5 | async-start | bytes 1081344 | tf_op jit(solution)/shard_map/all_gather | solution.py:9
  497.7 228.3 %all-gather.21.cloned.1.call-start = ((), (), s32[]{:S(2)}) async-start(), calls=%async_computation.6 | async-start | bytes 1081344 | tf_op jit(solution)/shard_map/all_gather | solution.py:9
  500.8 302.0 %all-gather.23.cloned.1.call-start = ((), (), s32[]{:S(2)}) async-start(), calls=%async_computation.7 | async-start | bytes 1081344 | tf_op jit(solution)/shard_map/all_gather | solution.py:9
  501.5 469.0 %all-reduce.5.cloned.1.call-start = ((), (), s32[]{:S(2)}) async-start(), calls=%async_computation.8 | async-start | bytes 262144 | tf_op jit(solution)/shard_map/psum | solution.py:26
  971.3 0.8 copy-start.2
Sparse Core Ops, SparseCore 0:
  16.7 75.5 all-gather.10
  95.5 73.8 all-gather.8
  172.5 73.8 all-gather.12
  248.9 73.8 all-gather.14
  351.9 138.5 all-reduce.6
  497.1 74.7 all-gather.16
  574.8 73.8 all-gather.18
  652.1 73.8 all-gather.20
  728.9 73.8 all-gather.22
  832.0 138.5 all-reduce.4
where the time goes:
time: 1020 us; the launch traced here: 1010 us
  waiting for transfers between devices  823 us (81%)
  other arithmetic  109 us (11%)
  blocking collectives  25.8 us (3%)
  local copies, waits for them, and re-layouts  21.5 us (2%)
  between operations  16 us (2%)
    all_gather x8, waiting for transfers between devices, carried_in(): pieces = jax.tree.map(lambda part: lax.all_gather(part, axis), value)  546 us
    psum x2, waiting for transfers between devices, spread(): return lax.psum(jnp.where(mine, x, jnp.zeros_like(x)), axis)  277 us
    select_n x124, other arithmetic, step(): jnp.where(position < mine, new, old)  98.6 us
    psum x1, blocking collectives, body(): density = lax.psum(density, 'col')  25.8 us
  transfers between devices with their start and end apart: 10, of which 10 were waited for; matrix products, arithmetic and copies ran while one was open for 6% of the time, Pallas kernels for 0%

commit v1 on v0

v1 whole, which is shorter than its diff:
```python
import functools

import jax
import jax.numpy as jnp
from jax import lax
from jax.experimental import pallas as pl
from jax.experimental.pallas import tpu as pltpu
from jax.sharding import PartitionSpec as P

F32, BF16 = jnp.float32, jnp.bfloat16
M = 64
HALF = M // 2
X = 16
LANES = 128
HALVES = 2
STEPS = 2
TILES = M // 8


def loop(count, step, carry=None):
    if carry is None:

        def plain(i, none):
            step(i)
            return none

        lax.fori_loop(0, count, plain, 0, unroll=True)
        return None
    return lax.fori_loop(0, count, step, carry, unroll=True)


def column(row):
    wide = jnp.broadcast_to(row, (M, M))
    here = lax.broadcasted_iota(jnp.int32, (M, M), 0) == lax.broadcasted_iota(jnp.int32, (M, M), 1)
    return jnp.sum(jnp.where(here, wide, 0.0), axis=1, keepdims=True)


def split(value):
    high = value.astype(BF16)
    low = (value - high.astype(F32)).astype(BF16)
    return high, low


def left_operand(weights):
    high, low = split(weights)
    return jnp.concatenate([high, high, low], axis=1)


def product(left, value):
    high, low = split(value)
    right = jnp.concatenate([high, low, high], axis=0)
    return jnp.dot(left, right, preferred_element_type=F32)


def kernel(
    cycle,
    sections,
    prop_ref,
    comp_ref,
    labels_ref,
    absorb_ref,
    ordin_ref,
    modes_ref,
    upwind_ref,
    decay_ref,
    out_ref,
    dens_ref,
    q_in,
    q_mid,
    q_out,
    comp,
    labels,
    absorb,
    ordin,
    modes,
    upwind,
    decay,
    rate,
    absorb_now,
    left_in,
    left_mid,
    left_mid_modes,
    left_out,
    inverse,
    ratio,
    unit,
    free,
    send_map,
    recv_map,
    send_unit,
    recv_unit,
    send_free,
    recv_free,
    prefix_unit,
    prefix_free,
    send_flow,
    recv_flow,
    send_early,
    recv_early,
    send_late,
    recv_late,
    dens,
    load_sem,
    q_sem,
    comp_sem,
    map_send,
    map_recv,
    unit_send,
    unit_recv,
    free_send,
    free_recv,
    flow_send,
    flow_recv,
    early_send,
    early_recv,
    late_send,
    late_recv,
    out_sem,
    dens_sem,
):
    me = lax.axis_index("gx")
    col = lax.axis_index("col")
    core = lax.rem(col, 2)
    my_tile = me // 4
    my_half = lax.rem(me, 4) // 2
    is_owner = lax.rem(me, 2) == lax.rem(my_tile + core, 2)

    small = [
        pltpu.make_async_copy(src, dst, load_sem.at[i])
        for i, (src, dst) in enumerate(
            (
                (absorb_ref, absorb),
                (upwind_ref, upwind),
                (labels_ref, labels),
                (ordin_ref, ordin),
                (modes_ref, modes),
                (decay_ref, decay),
            )
        )
    ]
    for copy in small:
        copy.start()
    q_load = [
        pltpu.make_async_copy(prop_ref.at[:, pl.ds(LANES * h, LANES)], q_in.at[h], q_sem.at[h])
        for h in range(HALVES)
    ]
    for copy in q_load:
        copy.start()
    comp_load = pltpu.make_async_copy(comp_ref, comp, comp_sem)
    comp_load.start()

    barrier = pltpu.get_barrier_semaphore()

    def greet_cycle(k, none):
        pl.semaphore_signal(barrier, inc=1, device_id={"gx": lax.rem(me + k, cycle)}, device_id_type=pl.DeviceIdType.MESH)
        return none

    def greet_sections(k, none):
        pl.semaphore_signal(barrier, inc=1, device_id={"col": lax.rem(col + k, sections)}, device_id_type=pl.DeviceIdType.MESH)
        return none

    lax.fori_loop(1, cycle, greet_cycle, 0)
    lax.fori_loop(1, sections, greet_sections, 0)

    for copy in small:
        copy.wait()

    rate[...] = jnp.broadcast_to(column(upwind[...]), (M, LANES))
    first = [labels[0, s] == 0 for s in range(STEPS)]
    for s in range(STEPS):
        absorb_now[s] = jnp.where(first[s], absorb[0], absorb[1])
    left_in[...] = left_operand(ordin[...])

    def coefficients(s, h):
        def one(i, carry):
            up, down = carry
            lanes = pl.ds(LANES * h, LANES)
            j = X - 1 - i
            rate_up, rate_down = rate[:HALF], rate[HALF:]
            inverse_up = 1.0 / (1.0 + rate_up + absorb_now[s, pl.ds(i, 1), lanes])
            inverse_down = 1.0 / (1.0 + rate_down + absorb_now[s, pl.ds(j, 1), lanes])
            ratio_up = rate_up * inverse_up
            ratio_down = rate_down * inverse_down
            up = up * ratio_up
            down = down * ratio_down
            inverse[s, h, i, :HALF] = inverse_up
            inverse[s, h, j, HALF:] = inverse_down
            ratio[s, h, i, :HALF] = ratio_up
            ratio[s, h, j, HALF:] = ratio_down
            unit[s, h, i, :HALF] = up
            unit[s, h, j, HALF:] = down
            return up, down

        ones = jnp.ones((HALF, LANES), F32)
        return loop(X, one, (ones, ones))

    def sweep(s, h):
        def one(i, carry):
            up, down = carry
            j = X - 1 - i
            up = free[s, h, i, :HALF] + ratio[s, h, i, :HALF] * up
            down = free[s, h, j, HALF:] + ratio[s, h, j, HALF:] * down
            free[s, h, i, :HALF] = up
            free[s, h, j, HALF:] = down
            return up, down

        zeros = jnp.zeros((HALF, LANES), F32)
        return loop(X, one, (zeros, zeros))

    def owner_of(t, h):
        return 4 * t + 2 * h + lax.rem(t + core, 2)

    def to_owners(source, target, send_sem, recv_sem, h):
        def one(t):
            owner = owner_of(t, h)

            @pl.when(owner != me)
            def _():
                pltpu.make_async_remote_copy(
                    src_ref=source.at[h, t],
                    dst_ref=target.at[me],
                    send_sem=send_sem,
                    recv_sem=recv_sem,
                    device_id={"gx": owner},
                    device_id_type=pl.DeviceIdType.MESH,
                ).start()

        loop(TILES, one)

        @pl.when(jnp.logical_and(is_owner, my_half == h))
        def _():
            target[me] = source[h, my_tile]

    def tile_rows(pair, t):
        up, down = pair
        rows = up if t < TILES // 2 else down
        base = 8 * (t % (TILES // 2))
        return rows[base : base + 8]

    for h in range(HALVES):
        units = coefficients(0, h)
        for t in range(TILES):
            send_map[h, t, 0] = tile_rows(units, t)
    for h in range(HALVES):
        q_load[h].wait()

        def sources(i):
            value = jnp.concatenate(
                [q_in[h, pl.ds(2 * i, M, stride=X), :], q_in[h, pl.ds(2 * i + 1, M, stride=X), :]], axis=1
            )
            result = product(left_in[...], value)
            free[0, h, 2 * i] = result[:, :LANES] * inverse[0, h, 2 * i]
            free[0, h, 2 * i + 1] = result[:, LANES:] * inverse[0, h, 2 * i + 1]

        loop(X // 2, sources)
        frees = sweep(0, h)
        for t in range(TILES):
            send_map[h, t, 1] = tile_rows(frees, t)
        if h == 0:
            pl.semaphore_wait(barrier, cycle + sections - 2)
        to_owners(send_map, recv_map, map_send, map_recv, h)

    for h in range(HALVES):
        units = coefficients(1, h)
        for t in range(TILES):
            send_unit[h, t] = tile_rows(units, t)
        to_owners(send_unit, recv_unit, unit_send, unit_recv, h)
    gained = []
    for s in range(STEPS):
        gain = jnp.where(first[s], decay[0:1], decay[1:2])
        gained.append(column(gain) * modes[...])
    left_mid[...] = left_operand(
        jnp.dot(ordin[...], gained[0], preferred_element_type=F32, precision=lax.Precision.HIGHEST)
    )
    left_mid_modes[...] = left_operand(gained[0])
    left_out[...] = left_operand(gained[1])

    def place(k):
        return jnp.where(my_tile < TILES // 2, k, cycle - 1 - k)

    def wait_for(ref, sem):
        pltpu.make_async_copy(ref, ref, sem).wait()

    def send_inflows(s, entry):
        def one(k):
            p = place(k)
            flow = prefix_unit[s, k] * entry + prefix_free[k]
            send_flow[s, p] = flow

            @pl.when(p != me)
            def _():
                pltpu.make_async_remote_copy(
                    src_ref=send_flow.at[s, p],
                    dst_ref=recv_flow.at[s, my_half, my_tile],
                    send_sem=flow_send.at[s],
                    recv_sem=flow_recv.at[s, my_half],
                    device_id={"gx": p},
                    device_id_type=pl.DeviceIdType.MESH,
                ).start()

        loop(cycle, one)
        recv_flow[s, my_half, my_tile] = send_flow[s, me]

    @pl.when(is_owner)
    def _():
        wait_for(recv_map.at[pl.ds(0, cycle - 1)], map_recv)

        def one(k, carry):
            whole_unit, whole_free = carry
            p = place(k)
            prefix_unit[0, k] = whole_unit
            prefix_free[k] = whole_free
            step_unit = recv_map[p, 0]
            return whole_unit * step_unit, step_unit * whole_free + recv_map[p, 1]

        ones, zeros = jnp.ones((8, LANES), F32), jnp.zeros((8, LANES), F32)
        whole_unit, whole_free = loop(cycle, one, (ones, zeros))
        send_inflows(0, whole_free / (1.0 - whole_unit))

    def wait_inflows(s, h):
        owns = jnp.logical_and(is_owner, my_half == h)

        @pl.when(owns)
        def _():
            wait_for(recv_flow.at[s, h, pl.ds(0, TILES - 1)], flow_recv.at[s, h])

        @pl.when(jnp.logical_not(owns))
        def _():
            wait_for(recv_flow.at[s, h], flow_recv.at[s, h])

    def swept(s, h, i, inflow):
        return free[s, h, i] + unit[s, h, i] * inflow

    for h in range(HALVES):
        wait_inflows(0, h)
        inflow = recv_flow[0, h].reshape(M, LANES)

        def sources(i):
            a, b = swept(0, h, 2 * i, inflow), swept(0, h, 2 * i + 1, inflow)
            free[0, h, 2 * i] = a
            free[0, h, 2 * i + 1] = b
            result = product(left_mid[...], jnp.concatenate([a, b], axis=1))
            free[1, h, 2 * i] = result[:, :LANES] * inverse[1, h, 2 * i]
            free[1, h, 2 * i + 1] = result[:, LANES:] * inverse[1, h, 2 * i + 1]

        loop(X // 2, sources)
        frees = sweep(1, h)
        for t in range(TILES):
            send_free[h, t] = tile_rows(frees, t)
        to_owners(send_free, recv_free, free_send, free_recv, h)

    def density(s, h, q):
        def one(i, total):
            rows = pl.ds(8 * X * i, 8 * X)
            term = q[h, rows, :] * comp[s, rows, pl.ds(LANES * h, LANES)].astype(F32)
            return total + jnp.sum(term.reshape(8, X, LANES), axis=0)

        return loop(M // 8, one, jnp.zeros((X, LANES), F32))

    def to_sections(source, target, send_sem, recv_sem):
        def one(k):
            pltpu.make_async_remote_copy(
                src_ref=source,
                dst_ref=target,
                send_sem=send_sem,
                recv_sem=recv_sem,
                device_id={"col": lax.rem(col + 1 + k, sections)},
                device_id_type=pl.DeviceIdType.MESH,
            ).start()

        loop(sections - 1, one)

    comp_load.wait()
    for h in range(HALVES):

        def middle(i):
            value = jnp.concatenate([free[0, h, 2 * i], free[0, h, 2 * i + 1]], axis=1)
            result = product(left_mid_modes[...], value)
            q_mid[h, pl.ds(2 * i, M, stride=X), :] = result[:, :LANES]
            q_mid[h, pl.ds(2 * i + 1, M, stride=X), :] = result[:, LANES:]

        loop(X // 2, middle)
        send_early[pl.ds(X * h, X)] = density(0, h, q_mid)
    for s in range(STEPS):
        send_early[pl.ds(2 * X + 8 * s, 8)] = jnp.broadcast_to(labels[0, s].astype(F32), (8, LANES))
    to_sections(send_early, recv_early.at[col], early_send, early_recv)
    recv_early[col] = send_early[...]

    @pl.when(is_owner)
    def _():
        wait_for(recv_unit.at[pl.ds(0, cycle - 1)], unit_recv)

        def units(k, whole_unit):
            prefix_unit[1, k] = whole_unit
            return whole_unit * recv_unit[place(k)]

        whole_unit = loop(cycle, units, jnp.ones((8, LANES), F32))
        wait_for(recv_free.at[pl.ds(0, cycle - 1)], free_recv)

        def one(k, whole_free):
            p = place(k)
            prefix_free[k] = whole_free
            return recv_unit[p] * whole_free + recv_free[p]

        whole_free = loop(cycle, one, jnp.zeros((8, LANES), F32))
        send_inflows(1, whole_free / (1.0 - whole_unit))

    q_store = [
        pltpu.make_async_copy(q_out.at[h], out_ref.at[:, pl.ds(LANES * h, LANES)], out_sem.at[h])
        for h in range(HALVES)
    ]
    for h in range(HALVES):
        wait_inflows(1, h)
        inflow = recv_flow[1, h].reshape(M, LANES)

        def last(i):
            value = jnp.concatenate([swept(1, h, 2 * i, inflow), swept(1, h, 2 * i + 1, inflow)], axis=1)
            result = product(left_out[...], value)
            q_out[h, pl.ds(2 * i, M, stride=X), :] = result[:, :LANES]
            q_out[h, pl.ds(2 * i + 1, M, stride=X), :] = result[:, LANES:]

        loop(X // 2, last)
        q_store[h].start()
        send_late[h] = density(1, h, q_out)
        to_sections(send_late.at[h], recv_late.at[h, col], late_send.at[h], late_recv.at[h])
        recv_late[h, col] = send_late[h]

    wait_for(recv_early.at[pl.ds(0, sections - 1)], early_recv)
    for h in range(HALVES):
        wait_for(recv_late.at[h, pl.ds(0, sections - 1)], late_recv.at[h])

        def one(c, carry):
            total_a, total_b = carry
            terms = (recv_early[c, pl.ds(X * h, X)], recv_late[h, c])
            for s in range(STEPS):
                label = recv_early[c, pl.ds(2 * X + 8 * s, 8)]
                is_a = jnp.concatenate([label, label], axis=0) == 0.0
                total_a = total_a + jnp.where(is_a, terms[s], 0.0)
                total_b = total_b + jnp.where(is_a, 0.0, terms[s])
            return total_a, total_b

        zeros = jnp.zeros((X, LANES), F32)
        total_a, total_b = loop(sections, one, (zeros, zeros))
        dens[0, :, pl.ds(LANES * h, LANES)] = total_a
        dens[1, :, pl.ds(LANES * h, LANES)] = total_b
    dens_store = pltpu.make_async_copy(dens, dens_ref, dens_sem)
    dens_store.start()

    for h in range(HALVES):
        owns = jnp.logical_and(is_owner, my_half == h)

        for count, when in ((TILES - 1, owns), (TILES, jnp.logical_not(owns))):

            @pl.when(when)
            def _():
                wait_for(send_map.at[h, pl.ds(0, count)], map_send)
                wait_for(send_unit.at[h, pl.ds(0, count)], unit_send)
                wait_for(send_free.at[h, pl.ds(0, count)], free_send)

    @pl.when(is_owner)
    def _():
        for s in range(STEPS):
            wait_for(send_flow.at[s, pl.ds(0, cycle - 1)], flow_send.at[s])

    wait_for(recv_early.at[pl.ds(0, sections - 1)], early_send)
    for h in range(HALVES):
        wait_for(recv_late.at[h, pl.ds(0, sections - 1)], late_send.at[h])
    for copy in q_store:
        copy.wait()
    dens_store.wait()


def body(propagator, complement, labels, absorption, to_ordinates, to_modes, upwind, mode_decay):
    cycle = lax.axis_size("gx")
    sections = lax.axis_size("col")
    rows, lines = M * X, HALVES * LANES
    dma = pltpu.SemaphoreType.DMA
    anywhere = pl.BlockSpec(memory_space=pl.ANY)
    left = pltpu.VMEM((M, 3 * M), BF16)
    cells = pltpu.VMEM((STEPS, HALVES, X, M, LANES), F32)
    scratch = [
        pltpu.VMEM((HALVES, rows, LANES), F32),
        pltpu.VMEM((HALVES, rows, LANES), F32),
        pltpu.VMEM((HALVES, rows, LANES), F32),
        pltpu.VMEM((STEPS, rows, lines), BF16),
        pltpu.SMEM((1, STEPS), jnp.int32),
        pltpu.VMEM((2, X, lines), F32),
        pltpu.VMEM((M, M), F32),
        pltpu.VMEM((M, M), F32),
        pltpu.VMEM((1, M), F32),
        pltpu.VMEM((2, M), F32),
        pltpu.VMEM((M, LANES), F32),
        pltpu.VMEM((STEPS, X, lines), F32),
        left,
        left,
        left,
        left,
        cells,
        cells,
        cells,
        cells,
        pltpu.VMEM((HALVES, TILES, 2, 8, LANES), F32),
        pltpu.VMEM((cycle, 2, 8, LANES), F32),
        pltpu.VMEM((HALVES, TILES, 8, LANES), F32),
        pltpu.VMEM((cycle, 8, LANES), F32),
        pltpu.VMEM((HALVES, TILES, 8, LANES), F32),
        pltpu.VMEM((cycle, 8, LANES), F32),
        pltpu.VMEM((STEPS, cycle, 8, LANES), F32),
        pltpu.VMEM((cycle, 8, LANES), F32),
        pltpu.VMEM((STEPS, cycle, 8, LANES), F32),
        pltpu.VMEM((STEPS, HALVES, TILES, 8, LANES), F32),
        pltpu.VMEM((3 * X, LANES), F32),
        pltpu.VMEM((sections, 3 * X, LANES), F32),
        pltpu.VMEM((HALVES, X, LANES), F32),
        pltpu.VMEM((HALVES, sections, X, LANES), F32),
        pltpu.VMEM((2, X, lines), F32),
        dma((6,)),
        dma((HALVES,)),
        dma,
        dma,
        dma,
        dma,
        dma,
        dma,
        dma,
        dma((STEPS,)),
        dma((STEPS, HALVES)),
        dma,
        dma,
        dma((HALVES,)),
        dma((HALVES,)),
        dma((HALVES,)),
        dma,
    ]
    propagated, density = pl.pallas_call(
        functools.partial(kernel, cycle, sections),
        out_shape=(
            jax.ShapeDtypeStruct((rows, lines), F32),
            jax.ShapeDtypeStruct((2, X, lines), F32),
        ),
        in_specs=[anywhere] * 8,
        out_specs=(anywhere, anywhere),
        scratch_shapes=scratch,
        compiler_params=pltpu.CompilerParams(
            collective_id=0, has_side_effects=True, vmem_limit_bytes=48 * 1024 * 1024
        ),
        name="contour_steps",
    )(
        propagator.reshape(rows, lines),
        complement.reshape(STEPS, rows, lines),
        labels,
        absorption,
        to_ordinates,
        to_modes,
        upwind.reshape(1, M),
        mode_decay,
    )
    return propagated.reshape(1, M, X, lines), density


def solution(mesh):
    in_specs = (
        P("col", None, "gx", None),
        P("col", None, None, "gx", None),
        P("col", None),
        P(None, "gx", None),
        P(),
        P(),
        P(),
        P(),
    )
    out_specs = (P("col", None, "gx", None), P(None, "gx", None))
    return jax.shard_map(body, mesh=mesh, in_specs=in_specs, out_specs=out_specs, check_vma=False)
```

time: 1020 us -> 53.2 us (0.05); the launches traced: 1010 us -> 52.8 us
  waiting for transfers between devices: 823 us -> 0 us
  other arithmetic: 109 us -> 0 us
  Pallas kernels: 0 us -> 45.2 us
  blocking collectives: 25.8 us -> 0 us
  between operations: 16 us -> 0.67 us
  local copies, waits for them, and re-layouts: 21.5 us -> 6.98 us
    all_gather x8 -> x0, waiting for transfers between devices: 546 us -> none  [carried_in(): pieces = jax.tree.map(lambda part: lax.all_gather(part, axis), value)]
    psum x2 -> x0, waiting for transfers between devices: 277 us -> none  [spread(): return lax.psum(jnp.where(mine, x, jnp.zeros_like(x)), axis)]
    select_n x132 -> x0, other arithmetic: 101 us -> none  [the longest x124 98.6 us: step(): jnp.where(position < mine, new, old)]
    pallas_call x0 -> x1, Pallas kernels: none -> 45.2 us  [body(): pl.pallas_call(functools.partial(kernel, cycle, sections), out_shape=(jax...]
    psum x1 -> x0, blocking collectives: 25.8 us -> none  [body(): density = lax.psum(density, 'col')]
  transfers between devices with their start and end apart: 10 -> 0, of which waited for: 10 -> 0; matrix products, arithmetic and copies ran while one was open for 6% -> 0% of each run, Pallas kernels for 0% -> 0%
where the time goes in v1:
time: 53.2 us; the launch traced here: 52.8 us
  Pallas kernels  45.2 us (85%)
  local copies, waits for them, and re-layouts  6.98 us (13%)
  between operations  0.67 us (1%)
    pallas_call x1, Pallas kernels, body(): pl.pallas_call(functools.partial(kernel, cycle, sections), out_shape=(jax...  45.2 us
    unnamed x18, local copies, waits for them, and re-layouts  6.98 us

profile of v1, /device:TPU:1, one launch (start us, length us, event | category | flops | bytes accessed | tf_op | source)
XLA Modules:
  0.0 52.8 jit_solution(3306454765234328251)
XLA Ops:
  0.6 0.0 copy-start.7
  0.6 0.0 copy-start.5
  0.7 0.0 copy-start.6
  0.7 0.6 %copy-done.7 = f32[64]{0:T(128)S(1)} copy-done((f32[64]{0:T(128)S(1)}, f32[64]{0:T(128)}, u32[]{:S(2)}) %copy-start.7) | copy-done | bytes 280
  1.3 0.0 copy-done.5
  1.3 0.0 copy-done.6
  1.3 0.0 copy-start
  1.3 1.2 %copy-done = f32[1,64,16,256]{3,2,1,0:T(8,128)S(1)} copy-done((f32[1,64,16,256]{3,2,1,0:T(8,128)S(1)}, f32[1,64,16,256]{3,2,1,0:T(8,128)}, u32[]{:S(2)}) %copy-start) | copy-done | bytes 1048600
  2.6 0.0 copy-start.1
  2.6 1.2 %copy-done.1 = bf16[1,2,64,16,256]{4,3,2,1,0:T(8,128)(2,1)S(1)} copy-done((bf16[1,2,64,16,256]{4,3,2,1,0:T(8,128)(2,1)S(1)}, bf16[1,2,64,16,256]{4,3,2,1,0:T(8,128)(2,1)}, u32[]{:S(2)}) %copy-start.1) | copy-done | bytes 1048600
  3.8 0.0 copy-start.2
  3.8 0.8 %copy-done.2 = f32[2,16,256]{2,1,0:T(8,128)S(1)} copy-done((f32[2,16,256]{2,1,0:T(8,128)S(1)}, f32[2,16,256]{2,1,0:T(8,128)}, u32[]{:S(2)}) %copy-start.2) | copy-done | bytes 32792
  4.5 0.0 copy-start.3
  4.5 0.8 %copy-done.3 = f32[64,64]{1,0:T(8,128)S(1)} copy-done((f32[64,64]{1,0:T(8,128)S(1)}, f32[64,64]{1,0:T(8,128)}, u32[]{:S(2)}) %copy-start.3) | copy-done | bytes 16408
  5.3 0.0 copy-start.4
  5.3 0.8 %copy-done.4 = f32[64,64]{1,0:T(8,128)S(1)} copy-done((f32[64,64]{1,0:T(8,128)S(1)}, f32[64,64]{1,0:T(8,128)}, u32[]{:S(2)}) %copy-start.4) | copy-done | bytes 16408
  6.1 45.2 %contour_steps.1 = (f32[1024,256]{1,0:T(8,128)S(1)}, f32[2,16,256]{2,1,0:T(8,128)S(1)}) custom-call(f32[1024,256]{1,0:T(8,128)S(1)} %bitcast.4, bf16[2,1024,256]{2,1,0:T(8,128)(2,1)S(1)} %bitcast.5, s32[1,2]{1,0:T(1,128)S(1)} %copy-done.6, f32[2,16,256]{2,1,0:T(8,128)S(1)} %copy-done.2, f32[64,64]{1,0:T(8,128)S(1)} %copy-done.3, f32[64,64]{1,0:T(8,128)S(1)} %copy-done.4, ...), custom_call_target="tpu_custom_call" | custom-call | tf_op jit(solution)/shard_map/contour_steps/pallas_call | solution.py:535
  51.2 1.0 %copy.12 = f32[1,64,16,256]{3,2,1,0:T(8,128)} copy(f32[1,64,16,256]{3,2,1,0:T(8,128)S(1)} %bitcast.6) | data formatting | bytes 2097152
  52.2 0.6 %copy.13 = f32[2,16,256]{2,1,0:T(8,128)} copy(f32[2,16,256]{2,1,0:T(8,128)S(1)} %get-tuple-element.9) | data formatting | bytes 65536
Async XLA Ops:
  0.6 0.7 %copy-start.7 = (f32[64]{0:T(128)S(1)}, f32[64]{0:T(128)}, u32[]{:S(2)}) copy-start(f32[64]{0:T(128)} %param.14) | copy-start | bytes 772
  0.6 0.7 %copy-start.5 = (f32[2,64]{1,0:T(2,128)S(1)}, f32[2,64]{1,0:T(2,128)}, u32[]{:S(2)}) copy-start(f32[2,64]{1,0:T(2,128)} %decay_ref.1) | copy-start | bytes 1540
  0.7 0.7 %copy-start.6 = (s32[1,2]{1,0:T(1,128)S(1)}, s32[1,2]{1,0:T(1,128)}, u32[]{:S(2)}) copy-start(s32[1,2]{1,0:T(1,128)} %labels_ref.1) | copy-start | bytes 28
  1.3 1.2 %copy-start = (f32[1,64,16,256]{3,2,1,0:T(8,128)S(1)}, f32[1,64,16,256]{3,2,1,0:T(8,128)}, u32[]{:S(2)}) copy-start(f32[1,64,16,256]{3,2,1,0:T(8,128)} %param.8) | copy-start | bytes 3145732
  2.6 1.2 %copy-start.1 = (bf16[1,2,64,16,256]{4,3,2,1,0:T(8,128)(2,1)S(1)}, bf16[1,2,64,16,256]{4,3,2,1,0:T(8,128)(2,1)}, u32[]{:S(2)}) copy-start(bf16[1,2,64,16,256]{4,3,2,1,0:T(8,128)(2,1)} %param.9) | copy-start | bytes 3145732
  3.8 0.8 %copy-start.2 = (f32[2,16,256]{2,1,0:T(8,128)S(1)}, f32[2,16,256]{2,1,0:T(8,128)}, u32[]{:S(2)}) copy-start(f32[2,16,256]{2,1,0:T(8,128)} %absorb_ref.1) | copy-start | bytes 98308
  4.5 0.8 %copy-start.3 = (f32[64,64]{1,0:T(8,128)S(1)}, f32[64,64]{1,0:T(8,128)}, u32[]{:S(2)}) copy-start(f32[64,64]{1,0:T(8,128)} %ordin_ref.1) | copy-start | bytes 49156
  5.3 0.8 %copy-start.4 = (f32[64,64]{1,0:T(8,128)S(1)}, f32[64,64]{1,0:T(8,128)}, u32[]{:S(2)}) copy-start(f32[64,64]{1,0:T(8,128)} %modes_ref.1) | copy-start | bytes 49156

commit v2 on v1

--- a/solution.py
+++ b/solution.py
@@ -15,6 +15,8 @@
 HALVES = 2
 STEPS = 2
 TILES = M // 8
+RING_Z, RING_Y, RING_X = 8, 4, 4
+FAR_Z, FAR_Y, FAR_X = (4, 3, 5, 2, 6, 1, 7, 0), (2, 1, 3, 0), (2, 1, 3, 0)
 
 
 def loop(count, step, carry=None):
@@ -121,9 +123,14 @@
     me = lax.axis_index("gx")
     col = lax.axis_index("col")
     core = lax.rem(col, 2)
-    my_tile = me // 4
-    my_half = lax.rem(me, 4) // 2
-    is_owner = lax.rem(me, 2) == lax.rem(my_tile + core, 2)
+    my_z, my_y, my_x = me // RING_Y, lax.rem(me, RING_Y), col // 2
+    is_owner = core == 1
+    parity = lax.rem(my_z + my_y, 2)
+    owns_here = jnp.logical_and(is_owner, parity == 1)
+    owns_other = jnp.logical_and(is_owner, parity == 0)
+    my_tile, my_half = my_z, my_y // 2
+    owner_col = col - core + 1
+    served_col = col - 1 + parity
 
     small = [
         pltpu.make_async_copy(src, dst, load_sem.at[i])
@@ -151,16 +158,47 @@
 
     barrier = pltpu.get_barrier_semaphore()
 
-    def greet_cycle(k, none):
-        pl.semaphore_signal(barrier, inc=1, device_id={"gx": lax.rem(me + k, cycle)}, device_id_type=pl.DeviceIdType.MESH)
-        return none
-
-    def greet_sections(k, none):
-        pl.semaphore_signal(barrier, inc=1, device_id={"col": lax.rem(col + k, sections)}, device_id_type=pl.DeviceIdType.MESH)
-        return none
-
-    lax.fori_loop(1, cycle, greet_cycle, 0)
-    lax.fori_loop(1, sections, greet_sections, 0)
+    def far_places():
+        for dz in FAR_Z:
+            for dy in FAR_Y:
+                yield RING_Y * lax.rem(my_z + dz, RING_Z) + lax.rem(my_y + dy, RING_Y), (dz, dy) == (0, 0)
+
+    def far_sections():
+        for dx in FAR_X:
+            for dc in range(2):
+                if (dx, dc) != (0, 0):
+                    yield 2 * lax.rem(my_x + dx, RING_X) + lax.rem(core + dc, 2)
+
+    def far_owners(halves=range(HALVES)):
+        for dz in FAR_Z:
+            for h in halves:
+                t = lax.rem(my_z + dz, RING_Z)
+                yield t, h, RING_Y * t + 2 * h + lax.rem(t + core, 2), dz == 0
+
+    def greet(place, section):
+        pl.semaphore_signal(
+            barrier, inc=1, device_id={"gx": place, "col": section}, device_id_type=pl.DeviceIdType.MESH
+        )
+
+    @pl.when(owns_here)
+    def _():
+        for place, here in far_places():
+            if not here:
+                greet(place, col)
+
+    @pl.when(owns_other)
+    def _():
+        for place, here in far_places():
+            greet(place, served_col)
+
+    @pl.when(jnp.logical_not(owns_here))
+    def _():
+        for t, h, owner, near in far_owners():
+            greet(owner, owner_col)
+
+    for section in far_sections():
+        greet(me, section)
+    greeted = jnp.where(owns_here, cycle - 1, jnp.where(owns_other, cycle + 2 * TILES, 2 * TILES)) + sections - 1
 
     for copy in small:
         copy.wait()
@@ -207,29 +245,29 @@
         zeros = jnp.zeros((HALF, LANES), F32)
         return loop(X, one, (zeros, zeros))
 
-    def owner_of(t, h):
-        return 4 * t + 2 * h + lax.rem(t + core, 2)
-
-    def to_owners(source, target, send_sem, recv_sem, h):
-        def one(t):
-            owner = owner_of(t, h)
-
-            @pl.when(owner != me)
-            def _():
+    def to_owners(source, target, send_sem, recv_sem, halves):
+        for t, h, owner, near in far_owners(halves):
+
+            def send(t=t, h=h, owner=owner):
                 pltpu.make_async_remote_copy(
                     src_ref=source.at[h, t],
                     dst_ref=target.at[me],
                     send_sem=send_sem,
                     recv_sem=recv_sem,
-                    device_id={"gx": owner},
+                    device_id={"gx": owner, "col": owner_col},
                     device_id_type=pl.DeviceIdType.MESH,
                 ).start()
 
-        loop(TILES, one)
-
-        @pl.when(jnp.logical_and(is_owner, my_half == h))
-        def _():
-            target[me] = source[h, my_tile]
+            if near:
+                pl.when(jnp.logical_not(jnp.logical_and(owns_here, h == my_half)))(send)
+            else:
+                send()
+
+        for h in halves:
+
+            @pl.when(jnp.logical_and(owns_here, my_half == h))
+            def _():
+                target[me] = source[h, my_tile]
 
     def tile_rows(pair, t):
         up, down = pair
@@ -242,29 +280,9 @@
         for t in range(TILES):
             send_map[h, t, 0] = tile_rows(units, t)
     for h in range(HALVES):
-        q_load[h].wait()
-
-        def sources(i):
-            value = jnp.concatenate(
-                [q_in[h, pl.ds(2 * i, M, stride=X), :], q_in[h, pl.ds(2 * i + 1, M, stride=X), :]], axis=1
-            )
-            result = product(left_in[...], value)
-            free[0, h, 2 * i] = result[:, :LANES] * inverse[0, h, 2 * i]
-            free[0, h, 2 * i + 1] = result[:, LANES:] * inverse[0, h, 2 * i + 1]
-
-        loop(X // 2, sources)
-        frees = sweep(0, h)
-        for t in range(TILES):
-            send_map[h, t, 1] = tile_rows(frees, t)
-        if h == 0:
-            pl.semaphore_wait(barrier, cycle + sections - 2)
-        to_owners(send_map, recv_map, map_send, map_recv, h)
-
-    for h in range(HALVES):
         units = coefficients(1, h)
         for t in range(TILES):
             send_unit[h, t] = tile_rows(units, t)
-        to_owners(send_unit, recv_unit, unit_send, unit_recv, h)
     gained = []
     for s in range(STEPS):
         gain = jnp.where(first[s], decay[0:1], decay[1:2])
@@ -275,39 +293,71 @@
     left_mid_modes[...] = left_operand(gained[0])
     left_out[...] = left_operand(gained[1])
 
-    def place(k):
+    for h in range(HALVES):
+        q_load[h].wait()
+
+        def sources(i):
+            value = jnp.concatenate(
+                [q_in[h, pl.ds(2 * i, M, stride=X), :], q_in[h, pl.ds(2 * i + 1, M, stride=X), :]], axis=1
+            )
+            result = product(left_in[...], value)
+            free[0, h, 2 * i] = result[:, :LANES] * inverse[0, h, 2 * i]
+            free[0, h, 2 * i + 1] = result[:, LANES:] * inverse[0, h, 2 * i + 1]
+
+        loop(X // 2, sources)
+        frees = sweep(0, h)
+        for t in range(TILES):
+            send_map[h, t, 1] = tile_rows(frees, t)
+    pl.semaphore_wait(barrier, greeted)
+    to_owners(send_map, recv_map, map_send, map_recv, range(HALVES))
+    to_owners(send_unit, recv_unit, unit_send, unit_recv, range(HALVES))
+
+    def along(k):
         return jnp.where(my_tile < TILES // 2, k, cycle - 1 - k)
 
     def wait_for(ref, sem):
         pltpu.make_async_copy(ref, ref, sem).wait()
 
+    def wait_for_tiles(ref, sem):
+        @pl.when(owns_here)
+        def _():
+            wait_for(ref.at[pl.ds(0, cycle - 1)], sem)
+
+        @pl.when(owns_other)
+        def _():
+            wait_for(ref, sem)
+
     def send_inflows(s, entry):
-        def one(k):
-            p = place(k)
-            flow = prefix_unit[s, k] * entry + prefix_free[k]
-            send_flow[s, p] = flow
-
-            @pl.when(p != me)
-            def _():
+        for p, here in far_places():
+            k = along(p)
+            send_flow[s, p] = prefix_unit[s, k] * entry + prefix_free[k]
+
+            def send(p=p):
                 pltpu.make_async_remote_copy(
                     src_ref=send_flow.at[s, p],
                     dst_ref=recv_flow.at[s, my_half, my_tile],
                     send_sem=flow_send.at[s],
                     recv_sem=flow_recv.at[s, my_half],
-                    device_id={"gx": p},
+                    device_id={"gx": p, "col": served_col},
                     device_id_type=pl.DeviceIdType.MESH,
                 ).start()
 
-        loop(cycle, one)
-        recv_flow[s, my_half, my_tile] = send_flow[s, me]
+            if here:
+                pl.when(owns_other)(send)
+            else:
+                send()
+
+        @pl.when(owns_here)
+        def _():
+            recv_flow[s, my_half, my_tile] = send_flow[s, me]
 
     @pl.when(is_owner)
     def _():
-        wait_for(recv_map.at[pl.ds(0, cycle - 1)], map_recv)
+        wait_for_tiles(recv_map, map_recv)
 
         def one(k, carry):
             whole_unit, whole_free = carry
-            p = place(k)
+            p = along(k)
             prefix_unit[0, k] = whole_unit
             prefix_free[k] = whole_free
             step_unit = recv_map[p, 0]
@@ -318,7 +368,7 @@
         send_inflows(0, whole_free / (1.0 - whole_unit))
 
     def wait_inflows(s, h):
-        owns = jnp.logical_and(is_owner, my_half == h)
+        owns = jnp.logical_and(owns_here, my_half == h)
 
         @pl.when(owns)
         def _():
@@ -347,7 +397,7 @@
         frees = sweep(1, h)
         for t in range(TILES):
             send_free[h, t] = tile_rows(frees, t)
-        to_owners(send_free, recv_free, free_send, free_recv, h)
+        to_owners(send_free, recv_free, free_send, free_recv, (h,))
 
     def density(s, h, q):
         def one(i, total):
@@ -358,17 +408,15 @@
         return loop(M // 8, one, jnp.zeros((X, LANES), F32))
 
     def to_sections(source, target, send_sem, recv_sem):
-        def one(k):
+        for section in far_sections():
             pltpu.make_async_remote_copy(
                 src_ref=source,
                 dst_ref=target,
                 send_sem=send_sem,
                 recv_sem=recv_sem,
-                device_id={"col": lax.rem(col + 1 + k, sections)},
+                device_id={"gx": me, "col": section},
                 device_id_type=pl.DeviceIdType.MESH,
             ).start()
-
-        loop(sections - 1, one)
 
     comp_load.wait()
     for h in range(HALVES):
@@ -388,17 +436,17 @@
 
     @pl.when(is_owner)
     def _():
-        wait_for(recv_unit.at[pl.ds(0, cycle - 1)], unit_recv)
+        wait_for_tiles(recv_unit, unit_recv)
 
         def units(k, whole_unit):
             prefix_unit[1, k] = whole_unit
-            return whole_unit * recv_unit[place(k)]
+            return whole_unit * recv_unit[along(k)]
 
         whole_unit = loop(cycle, units, jnp.ones((8, LANES), F32))
-        wait_for(recv_free.at[pl.ds(0, cycle - 1)], free_recv)
+        wait_for_tiles(recv_free, free_recv)
 
         def one(k, whole_free):
-            p = place(k)
+            p = along(k)
             prefix_free[k] = whole_free
             return recv_unit[p] * whole_free + recv_free[p]
 
@@ -447,7 +495,7 @@
     dens_store.start()
 
     for h in range(HALVES):
-        owns = jnp.logical_and(is_owner, my_half == h)
+        owns = jnp.logical_and(owns_here, my_half == h)
 
         for count, when in ((TILES - 1, owns), (TILES, jnp.logical_not(owns))):
 
@@ -457,10 +505,8 @@
                 wait_for(send_unit.at[h, pl.ds(0, count)], unit_send)
                 wait_for(send_free.at[h, pl.ds(0, count)], free_send)
 
-    @pl.when(is_owner)
-    def _():
-        for s in range(STEPS):
-            wait_for(send_flow.at[s, pl.ds(0, cycle - 1)], flow_send.at[s])
+    for s in range(STEPS):
+        wait_for_tiles(send_flow.at[s], flow_send.at[s])
 
     wait_for(recv_early.at[pl.ds(0, sections - 1)], early_send)
     for h in range(HALVES):
@@ -546,14 +592,19 @@
         ),
         name="contour_steps",
     )(
-        propagator.reshape(rows, lines),
-        complement.reshape(STEPS, rows, lines),
-        labels,
-        absorption,
-        to_ordinates,
-        to_modes,
-        upwind.reshape(1, M),
-        mode_decay,
+        *(
+            pltpu.with_memory_space_constraint(operand, pltpu.HBM)
+            for operand in (
+                propagator.reshape(rows, lines),
+                complement.reshape(STEPS, rows, lines),
+                labels,
+                absorption,
+                to_ordinates,
+                to_modes,
+                upwind.reshape(1, M),
+                mode_decay,
+            )
+        )
     )
     return propagated.reshape(1, M, X, lines), density
 

time: 53.2 us -> 41.5 us (0.78)
  Pallas kernels: 45.2 us -> 39.2 us
  local copies, waits for them, and re-layouts: 6.98 us -> 1.59 us
    pallas_call x1, Pallas kernels: 45.2 us -> 39.2 us  [body(): pl.pallas_call(functools.partial(kernel, cycle, sections), out_shape=(jax...]
    unnamed x18 -> x2, local copies, waits for them, and re-layouts: 6.98 us -> 1.59 us
where the time goes in v2:
time: 41.5 us; the launch traced here: 41.4 us
  Pallas kernels  39.2 us (94%)
  local copies, waits for them, and re-layouts  1.59 us (4%)
  between operations  0.64 us (2%)
    pallas_call x1, Pallas kernels, body(): pl.pallas_call(functools.partial(kernel, cycle, sections), out_shape=(jax...  39.2 us
    unnamed x2, local copies, waits for them, and re-layouts  1.59 us

profile of v2, /device:TPU:1, one launch (start us, length us, event | category | flops | bytes accessed | tf_op | source)
XLA Modules:
  0.0 41.4 jit_solution(7977942291678474256)
XLA Ops:
  0.6 39.2 %contour_steps.1 = (f32[1024,256]{1,0:T(8,128)S(1)}, f32[2,16,256]{2,1,0:T(8,128)S(1)}) custom-call(f32[1024,256]{1,0:T(8,128)} %bitcast.5, bf16[2,1024,256]{2,1,0:T(8,128)(2,1)} %bitcast.6, s32[1,2]{1,0:T(1,128)} %labels_ref.1, f32[2,16,256]{2,1,0:T(8,128)} %absorb_ref.1, f32[64,64]{1,0:T(8,128)} %ordin_ref.1, f32[64,64]{1,0:T(8,128)} %modes_ref.1, ...), custom_call_target="tpu_custom_call" | custom-call | tf_op jit(solution)/shard_map/contour_steps/pallas_call | solution.py:581
  39.9 1.0 %copy.12 = f32[1,64,16,256]{3,2,1,0:T(8,128)} copy(f32[1,64,16,256]{3,2,1,0:T(8,128)S(1)} %bitcast.4) | data formatting | bytes 2097152
  40.8 0.6 %copy.13 = f32[2,16,256]{2,1,0:T(8,128)} copy(f32[2,16,256]{2,1,0:T(8,128)S(1)} %get-tuple-element.9) | data formatting | bytes 65536

commit v3 on v2

--- a/solution.py
+++ b/solution.py
@@ -83,6 +83,7 @@
     left_mid,
     left_mid_modes,
     left_out,
+    left_comp,
     inverse,
     ratio,
     unit,
@@ -101,7 +102,9 @@
     recv_early,
     send_late,
     recv_late,
-    dens,
+    weight,
+    comp_wide,
+    comp_ordin,
     load_sem,
     q_sem,
     comp_sem,
@@ -118,7 +121,6 @@
     late_send,
     late_recv,
     out_sem,
-    dens_sem,
 ):
     me = lax.axis_index("gx")
     col = lax.axis_index("col")
@@ -131,6 +133,50 @@
     my_tile, my_half = my_z, my_y // 2
     owner_col = col - core + 1
     served_col = col - 1 + parity
+
+    barrier = pltpu.get_barrier_semaphore()
+
+    def far_places():
+        for dz in FAR_Z:
+            for dy in FAR_Y:
+                yield RING_Y * lax.rem(my_z + dz, RING_Z) + lax.rem(my_y + dy, RING_Y), (dz, dy) == (0, 0)
+
+    def far_sections():
+        for dx in FAR_X:
+            for dc in range(2):
+                if (dx, dc) != (0, 0):
+                    yield 2 * lax.rem(my_x + dx, RING_X) + lax.rem(core + dc, 2)
+
+    def far_owners(halves=range(HALVES)):
+        for dz in FAR_Z:
+            for h in halves:
+                t = lax.rem(my_z + dz, RING_Z)
+                yield t, h, RING_Y * t + 2 * h + lax.rem(t + core, 2), dz == 0
+
+    def greet(place, section):
+        pl.semaphore_signal(
+            barrier, inc=1, device_id={"gx": place, "col": section}, device_id_type=pl.DeviceIdType.MESH
+        )
+
+    @pl.when(owns_here)
+    def _():
+        for place, here in far_places():
+            if not here:
+                greet(place, col)
+
+    @pl.when(owns_other)
+    def _():
+        for place, here in far_places():
+            greet(place, served_col)
+
+    @pl.when(jnp.logical_not(owns_here))
+    def _():
+        for t, h, owner, near in far_owners():
+            greet(owner, owner_col)
+
+    for section in far_sections():
+        greet(me, section)
+    greeted = jnp.where(owns_here, cycle - 1, jnp.where(owns_other, cycle + 2 * TILES, 2 * TILES)) + sections - 1
 
     small = [
         pltpu.make_async_copy(src, dst, load_sem.at[i])
@@ -156,50 +202,6 @@
     comp_load = pltpu.make_async_copy(comp_ref, comp, comp_sem)
     comp_load.start()
 
-    barrier = pltpu.get_barrier_semaphore()
-
-    def far_places():
-        for dz in FAR_Z:
-            for dy in FAR_Y:
-                yield RING_Y * lax.rem(my_z + dz, RING_Z) + lax.rem(my_y + dy, RING_Y), (dz, dy) == (0, 0)
-
-    def far_sections():
-        for dx in FAR_X:
-            for dc in range(2):
-                if (dx, dc) != (0, 0):
-                    yield 2 * lax.rem(my_x + dx, RING_X) + lax.rem(core + dc, 2)
-
-    def far_owners(halves=range(HALVES)):
-        for dz in FAR_Z:
-            for h in halves:
-                t = lax.rem(my_z + dz, RING_Z)
-                yield t, h, RING_Y * t + 2 * h + lax.rem(t + core, 2), dz == 0
-
-    def greet(place, section):
-        pl.semaphore_signal(
-            barrier, inc=1, device_id={"gx": place, "col": section}, device_id_type=pl.DeviceIdType.MESH
-        )
-
-    @pl.when(owns_here)
-    def _():
-        for place, here in far_places():
-            if not here:
-                greet(place, col)
-
-    @pl.when(owns_other)
-    def _():
-        for place, here in far_places():
-            greet(place, served_col)
-
-    @pl.when(jnp.logical_not(owns_here))
-    def _():
-        for t, h, owner, near in far_owners():
-            greet(owner, owner_col)
-
-    for section in far_sections():
-        greet(me, section)
-    greeted = jnp.where(owns_here, cycle - 1, jnp.where(owns_other, cycle + 2 * TILES, 2 * TILES)) + sections - 1
-
     for copy in small:
         copy.wait()
 
@@ -236,14 +238,25 @@
         def one(i, carry):
             up, down = carry
             j = X - 1 - i
-            up = free[s, h, i, :HALF] + ratio[s, h, i, :HALF] * up
-            down = free[s, h, j, HALF:] + ratio[s, h, j, HALF:] * down
+            up = free[s, h, i, :HALF] * inverse[s, h, i, :HALF] + ratio[s, h, i, :HALF] * up
+            down = free[s, h, j, HALF:] * inverse[s, h, j, HALF:] + ratio[s, h, j, HALF:] * down
             free[s, h, i, :HALF] = up
             free[s, h, j, HALF:] = down
             return up, down
 
         zeros = jnp.zeros((HALF, LANES), F32)
         return loop(X, one, (zeros, zeros))
+
+    def weights(h):
+        def one(i, carry):
+            up, down = carry
+            j = X - 1 - i
+            weight[h, j, :HALF] = inverse[1, h, j, :HALF] * up
+            weight[h, i, HALF:] = inverse[1, h, i, HALF:] * down
+            return up * ratio[1, h, j, :HALF], down * ratio[1, h, i, HALF:]
+
+        ones = jnp.ones((HALF, LANES), F32)
+        loop(X, one, (ones, ones))
 
     def to_owners(source, target, send_sem, recv_sem, halves):
         for t, h, owner, near in far_owners(halves):
@@ -292,6 +305,7 @@
     )
     left_mid_modes[...] = left_operand(gained[0])
     left_out[...] = left_operand(gained[1])
+    left_comp[...] = jnp.concatenate(split(gained[1].T), axis=1)
 
     for h in range(HALVES):
         q_load[h].wait()
@@ -301,8 +315,8 @@
                 [q_in[h, pl.ds(2 * i, M, stride=X), :], q_in[h, pl.ds(2 * i + 1, M, stride=X), :]], axis=1
             )
             result = product(left_in[...], value)
-            free[0, h, 2 * i] = result[:, :LANES] * inverse[0, h, 2 * i]
-            free[0, h, 2 * i + 1] = result[:, LANES:] * inverse[0, h, 2 * i + 1]
+            free[0, h, 2 * i] = result[:, :LANES]
+            free[0, h, 2 * i + 1] = result[:, LANES:]
 
         loop(X // 2, sources)
         frees = sweep(0, h)
@@ -311,6 +325,27 @@
     pl.semaphore_wait(barrier, greeted)
     to_owners(send_map, recv_map, map_send, map_recv, range(HALVES))
     to_owners(send_unit, recv_unit, unit_send, unit_recv, range(HALVES))
+
+    for h in range(HALVES):
+        weights(h)
+    comp_load.wait()
+    for h in range(HALVES):
+
+        def widen(i):
+            rows = pl.ds(8 * X * i, 8 * X)
+            comp_wide[h, rows] = comp[1, rows, pl.ds(LANES * h, LANES)].astype(F32)
+
+        loop(M // 8, widen)
+
+        def to_ordinates(i):
+            value = jnp.concatenate(
+                [comp_wide[h, pl.ds(2 * i, M, stride=X), :], comp_wide[h, pl.ds(2 * i + 1, M, stride=X), :]], axis=1
+            ).astype(BF16)
+            result = jnp.dot(left_comp[...], jnp.concatenate([value, value], axis=0), preferred_element_type=F32)
+            comp_ordin[h, 2 * i] = result[:, :LANES]
+            comp_ordin[h, 2 * i + 1] = result[:, LANES:]
+
+        loop(X // 2, to_ordinates)
 
     def along(k):
         return jnp.where(my_tile < TILES // 2, k, cycle - 1 - k)
@@ -385,18 +420,18 @@
         wait_inflows(0, h)
         inflow = recv_flow[0, h].reshape(M, LANES)
 
-        def sources(i):
+        def sources(i, outflow):
             a, b = swept(0, h, 2 * i, inflow), swept(0, h, 2 * i + 1, inflow)
             free[0, h, 2 * i] = a
             free[0, h, 2 * i + 1] = b
             result = product(left_mid[...], jnp.concatenate([a, b], axis=1))
-            free[1, h, 2 * i] = result[:, :LANES] * inverse[1, h, 2 * i]
-            free[1, h, 2 * i + 1] = result[:, LANES:] * inverse[1, h, 2 * i + 1]
-
-        loop(X // 2, sources)
-        frees = sweep(1, h)
-        for t in range(TILES):
-            send_free[h, t] = tile_rows(frees, t)
+            a, b = result[:, :LANES], result[:, LANES:]
+            free[1, h, 2 * i] = a
+            free[1, h, 2 * i + 1] = b
+            return outflow + weight[h, 2 * i] * a + weight[h, 2 * i + 1] * b
+
+        outflow = loop(X // 2, sources, jnp.zeros((M, LANES), F32))
+        send_free[h] = outflow.reshape(TILES, 8, LANES)
         to_owners(send_free, recv_free, free_send, free_recv, (h,))
 
     def density(s, h, q):
@@ -418,7 +453,8 @@
                 device_id_type=pl.DeviceIdType.MESH,
             ).start()
 
-    comp_load.wait()
+    for h in range(HALVES):
+        sweep(1, h)
     for h in range(HALVES):
 
         def middle(i):
@@ -453,46 +489,54 @@
         whole_free = loop(cycle, one, jnp.zeros((8, LANES), F32))
         send_inflows(1, whole_free / (1.0 - whole_unit))
 
+    for h in range(HALVES):
+        wait_inflows(1, h)
+        inflow = recv_flow[1, h].reshape(M, LANES)
+
+        def last_density(i):
+            solved = swept(1, h, i, inflow)
+            free[1, h, i] = solved
+            send_late[h, pl.ds(i, 1)] = jnp.sum(solved * comp_ordin[h, i], axis=0, keepdims=True)
+
+        loop(X, last_density)
+        to_sections(send_late.at[h], recv_late.at[h, col], late_send.at[h], late_recv.at[h])
+        recv_late[h, col] = send_late[h]
     q_store = [
         pltpu.make_async_copy(q_out.at[h], out_ref.at[:, pl.ds(LANES * h, LANES)], out_sem.at[h])
         for h in range(HALVES)
     ]
     for h in range(HALVES):
-        wait_inflows(1, h)
-        inflow = recv_flow[1, h].reshape(M, LANES)
 
         def last(i):
-            value = jnp.concatenate([swept(1, h, 2 * i, inflow), swept(1, h, 2 * i + 1, inflow)], axis=1)
+            value = jnp.concatenate([free[1, h, 2 * i], free[1, h, 2 * i + 1]], axis=1)
             result = product(left_out[...], value)
             q_out[h, pl.ds(2 * i, M, stride=X), :] = result[:, :LANES]
             q_out[h, pl.ds(2 * i + 1, M, stride=X), :] = result[:, LANES:]
 
         loop(X // 2, last)
         q_store[h].start()
-        send_late[h] = density(1, h, q_out)
-        to_sections(send_late.at[h], recv_late.at[h, col], late_send.at[h], late_recv.at[h])
-        recv_late[h, col] = send_late[h]
 
     wait_for(recv_early.at[pl.ds(0, sections - 1)], early_recv)
-    for h in range(HALVES):
-        wait_for(recv_late.at[h, pl.ds(0, sections - 1)], late_recv.at[h])
-
+
+    def add_densities(carry, terms, s):
         def one(c, carry):
             total_a, total_b = carry
-            terms = (recv_early[c, pl.ds(X * h, X)], recv_late[h, c])
-            for s in range(STEPS):
-                label = recv_early[c, pl.ds(2 * X + 8 * s, 8)]
-                is_a = jnp.concatenate([label, label], axis=0) == 0.0
-                total_a = total_a + jnp.where(is_a, terms[s], 0.0)
-                total_b = total_b + jnp.where(is_a, 0.0, terms[s])
-            return total_a, total_b
-
-        zeros = jnp.zeros((X, LANES), F32)
-        total_a, total_b = loop(sections, one, (zeros, zeros))
-        dens[0, :, pl.ds(LANES * h, LANES)] = total_a
-        dens[1, :, pl.ds(LANES * h, LANES)] = total_b
-    dens_store = pltpu.make_async_copy(dens, dens_ref, dens_sem)
-    dens_store.start()
+            label = recv_early[c, pl.ds(2 * X + 8 * s, 8)]
+            is_a = jnp.concatenate([label, label], axis=0) == 0.0
+            term = terms(c)
+            return total_a + jnp.where(is_a, term, 0.0), total_b + jnp.where(is_a, 0.0, term)
+
+        return loop(sections, one, carry)
+
+    zeros = jnp.zeros((X, LANES), F32)
+    early = [
+        add_densities((zeros, zeros), lambda c, h=h: recv_early[c, pl.ds(X * h, X)], 0) for h in range(HALVES)
+    ]
+    for h in range(HALVES):
+        wait_for(recv_late.at[h, pl.ds(0, sections - 1)], late_recv.at[h])
+        total_a, total_b = add_densities(early[h], lambda c, h=h: recv_late[h, c], 1)
+        dens_ref[0, :, pl.ds(LANES * h, LANES)] = total_a
+        dens_ref[1, :, pl.ds(LANES * h, LANES)] = total_b
 
     for h in range(HALVES):
         owns = jnp.logical_and(owns_here, my_half == h)
@@ -513,7 +557,21 @@
         wait_for(recv_late.at[h, pl.ds(0, sections - 1)], late_send.at[h])
     for copy in q_store:
         copy.wait()
-    dens_store.wait()
+
+
+STORES = 4
+
+
+def store(q_ref, dens_ref, q_out, dens_out, sem):
+    part = M * X // STORES
+    copies = [pltpu.make_async_copy(dens_ref, dens_out, sem.at[STORES])]
+    for i in range(STORES):
+        rows = pl.ds(part * i, part)
+        copies.append(pltpu.make_async_copy(q_ref.at[rows], q_out.at[rows], sem.at[i]))
+    for copy in copies:
+        copy.start()
+    for copy in copies:
+        copy.wait()
 
 
 def body(propagator, complement, labels, absorption, to_ordinates, to_modes, upwind, mode_decay):
@@ -524,6 +582,7 @@
     anywhere = pl.BlockSpec(memory_space=pl.ANY)
     left = pltpu.VMEM((M, 3 * M), BF16)
     cells = pltpu.VMEM((STEPS, HALVES, X, M, LANES), F32)
+    halves_cells = pltpu.VMEM((HALVES, X, M, LANES), F32)
     scratch = [
         pltpu.VMEM((HALVES, rows, LANES), F32),
         pltpu.VMEM((HALVES, rows, LANES), F32),
@@ -541,6 +600,7 @@
         left,
         left,
         left,
+        pltpu.VMEM((M, 2 * M), BF16),
         cells,
         cells,
         cells,
@@ -559,7 +619,9 @@
         pltpu.VMEM((sections, 3 * X, LANES), F32),
         pltpu.VMEM((HALVES, X, LANES), F32),
         pltpu.VMEM((HALVES, sections, X, LANES), F32),
-        pltpu.VMEM((2, X, lines), F32),
+        halves_cells,
+        pltpu.VMEM((HALVES, rows, LANES), F32),
+        halves_cells,
         dma((6,)),
         dma((HALVES,)),
         dma,
@@ -576,7 +638,6 @@
         dma((HALVES,)),
         dma((HALVES,)),
         dma((HALVES,)),
-        dma,
     ]
     propagated, density = pl.pallas_call(
         functools.partial(kernel, cycle, sections),
@@ -585,7 +646,7 @@
             jax.ShapeDtypeStruct((2, X, lines), F32),
         ),
         in_specs=[anywhere] * 8,
-        out_specs=(anywhere, anywhere),
+        out_specs=(anywhere, pl.BlockSpec(memory_space=pltpu.VMEM)),
         scratch_shapes=scratch,
         compiler_params=pltpu.CompilerParams(
             collective_id=0, has_side_effects=True, vmem_limit_bytes=48 * 1024 * 1024
@@ -606,6 +667,18 @@
             )
         )
     )
+    propagated, density = pl.pallas_call(
+        store,
+        out_shape=(
+            jax.ShapeDtypeStruct((rows, lines), F32),
+            jax.ShapeDtypeStruct((2, X, lines), F32),
+        ),
+        in_specs=[anywhere] * 2,
+        out_specs=(anywhere, anywhere),
+        scratch_shapes=[dma((STORES + 1,))],
+        compiler_params=pltpu.CompilerParams(vmem_limit_bytes=1024 * 1024),
+        name="store_results",
+    )(propagated, density)
     return propagated.reshape(1, M, X, lines), density
 
 

time: 41.5 us -> 40.5 us (0.976)
  local copies, waits for them, and re-layouts: 1.59 us -> 0 us
  Pallas kernels: 39.2 us -> 39.8 us
    unnamed x2 -> x0, local copies, waits for them, and re-layouts: 1.59 us -> none
    pallas_call x0 -> x1, Pallas kernels: none -> 1.02 us  [body(): pl.pallas_call(store, out_shape=(jax.ShapeDtypeStruct((rows, lines), F32)...]
    pallas_call x1, Pallas kernels: 39.2 us -> 38.8 us  [body(): pl.pallas_call(functools.partial(kernel, cycle, sections), out_shape=(jax...]
where the time goes in v3:
time: 40.5 us; the launch traced here: 40.4 us
  Pallas kernels  39.8 us (98%)
  between operations  0.64 us (2%)
    pallas_call x1, Pallas kernels, body(): pl.pallas_call(functools.partial(kernel, cycle, sections), out_shape=(jax...  38.8 us
    pallas_call x1, Pallas kernels, body(): pl.pallas_call(store, out_shape=(jax.ShapeDtypeStruct((rows, lines), F32)...  1.02 us

profile of v3, /device:TPU:1, one launch (start us, length us, event | category | flops | bytes accessed | tf_op | source)
XLA Modules:
  0.0 40.4 jit_solution(2143658003076273985)
XLA Ops:
  0.6 38.8 %contour_steps.1 = (f32[1024,256]{1,0:T(8,128)S(1)}, f32[2,16,256]{2,1,0:T(8,128)S(1)}) custom-call(f32[1024,256]{1,0:T(8,128)} %bitcast.4, bf16[2,1024,256]{2,1,0:T(8,128)(2,1)} %bitcast.5, s32[1,2]{1,0:T(1,128)} %labels_ref.1, f32[2,16,256]{2,1,0:T(8,128)} %absorb_ref.1, f32[64,64]{1,0:T(8,128)} %ordin_ref.1, f32[64,64]{1,0:T(8,128)} %modes_ref.1, ...), custom_call_target="tpu_custom_call" | custom-call | tf_op jit(solution)/shard_map/contour_steps/pallas_call | solution.py:642
  39.4 1.0 %store_results.1 = (f32[1024,256]{1,0:T(8,128)}, f32[2,16,256]{2,1,0:T(8,128)}) custom-call(f32[1024,256]{1,0:T(8,128)S(1)} %get-tuple-element.6.q_ref, f32[2,16,256]{2,1,0:T(8,128)S(1)} %get-tuple-element.7.dens_ref), custom_call_target="tpu_custom_call" | custom-call | tf_op jit(solution)/shard_map/store_results/pallas_call | solution.py:670

commit v4 on v3

v4 whole, which is shorter than its diff:
```python
import jax
import jax.numpy as jnp
from jax import lax
from jax.experimental import pallas as pl
from jax.experimental.pallas import tpu as pltpu
from jax.sharding import PartitionSpec as P

F32, BF16 = jnp.float32, jnp.bfloat16
M = 64
HALF = M // 2
X = 16
LANES = 128
HALVES = 2
STEPS = 2
CYCLE, SECTIONS = 32, 8
OWN = 8
ROWS = CYCLE * OWN
RING_Z, RING_Y, RING_X = 8, 4, 4
FAR_Z, FAR_Y, FAR_X = (4, 3, 5, 2, 6, 1, 7, 0), (2, 1, 3, 0), (2, 1, 3, 0)
STORES = 4


def loop(count, step, carry=None):
    if carry is None:

        def plain(i, none):
            step(i)
            return none

        lax.fori_loop(0, count, plain, 0, unroll=True)
        return None
    return lax.fori_loop(0, count, step, carry, unroll=True)


def column(row):
    wide = jnp.broadcast_to(row, (M, M))
    here = lax.broadcasted_iota(jnp.int32, (M, M), 0) == lax.broadcasted_iota(jnp.int32, (M, M), 1)
    return jnp.sum(jnp.where(here, wide, 0.0), axis=1, keepdims=True)


def split(value):
    high = value.astype(BF16)
    low = (value - high.astype(F32)).astype(BF16)
    return high, low


def left_operand(weights):
    high, low = split(weights)
    return jnp.concatenate([high, high, low], axis=1)


def product(left, value):
    high, low = split(value)
    right = jnp.concatenate([high, low, high], axis=0)
    return jnp.dot(left, right, preferred_element_type=F32)


def wait_for(ref, sem):
    pltpu.make_async_copy(ref, ref, sem).wait()


def kernel(
    prop_ref,
    comp_ref,
    labels_ref,
    absorb_ref,
    ordin_ref,
    modes_ref,
    upwind_ref,
    decay_ref,
    out_ref,
    dens_ref,
    q_in,
    q_out,
    comp,
    labels,
    absorb,
    ordin,
    modes,
    upwind,
    decay,
    rate,
    absorb_now,
    left_in,
    left_mid,
    left_out,
    left_comp,
    inverse,
    ratio,
    unit,
    free,
    weight,
    comp_wide,
    comp_ordin,
    turned,
    send_absorb,
    recv_absorb,
    own_wide,
    own_absorb,
    own_inverse,
    own_ratio,
    own_unit,
    own_weight,
    send_out,
    recv_out,
    own_factor,
    prefix_unit,
    prefix_free,
    own_extra,
    send_flow,
    recv_flow,
    send_early,
    recv_early,
    send_late,
    recv_late,
    load_sem,
    q_sem,
    comp_sem,
    absorb_send,
    absorb_recv,
    out_send,
    out_recv,
    flow_send,
    flow_recv,
    early_send,
    early_recv,
    late_send,
    late_recv,
    store_sem,
):
    me = lax.axis_index("gx")
    col = lax.axis_index("col")
    core = lax.rem(col, 2)
    my_z, my_y, my_x = me // RING_Y, lax.rem(me, RING_Y), col // 2

    def far_places():
        for dz in FAR_Z:
            for dy in FAR_Y:
                if (dz, dy) != (0, 0):
                    yield RING_Y * lax.rem(my_z + dz, RING_Z) + lax.rem(my_y + dy, RING_Y)

    def far_sections():
        for dx in FAR_X:
            for dc in range(2):
                if (dx, dc) != (0, 0):
                    yield 2 * lax.rem(my_x + dx, RING_X) + lax.rem(core + dc, 2)

    barrier = pltpu.get_barrier_semaphore()

    def greet(place, section):
        pl.semaphore_signal(
            barrier, inc=1, device_id={"gx": place, "col": section}, device_id_type=pl.DeviceIdType.MESH
        )

    for place in far_places():
        greet(place, col)
    for section in far_sections():
        greet(me, section)

    small = [
        pltpu.make_async_copy(src, dst, load_sem.at[i])
        for i, (src, dst) in enumerate(
            (
                (absorb_ref, absorb),
                (upwind_ref, upwind),
                (labels_ref, labels),
                (ordin_ref, ordin),
                (modes_ref, modes),
                (decay_ref, decay),
            )
        )
    ]
    for copy in small:
        copy.start()
    q_load = [
        pltpu.make_async_copy(prop_ref.at[:, pl.ds(LANES * h, LANES)], q_in.at[h], q_sem.at[h])
        for h in range(HALVES)
    ]
    for copy in q_load:
        copy.start()
    comp_load = pltpu.make_async_copy(comp_ref, comp, comp_sem)
    comp_load.start()
    for copy in small:
        copy.wait()

    rate[...] = jnp.broadcast_to(column(upwind[...]), (M, LANES))
    first = [labels[0, s] == 0 for s in range(STEPS)]
    for s in range(STEPS):
        absorb_now[s] = jnp.where(first[s], absorb[0], absorb[1])
    left_in[...] = left_operand(ordin[...])

    def coefficients(rows, h, inverse, ratio, unit):
        def one(i, carry):
            up, down = carry
            lanes = pl.ds(LANES * h, LANES)
            j = X - 1 - i
            rate_up, rate_down = rate[:HALF], rate[HALF:]
            inverse_up = 1.0 / (1.0 + rate_up + rows[pl.ds(i, 1), lanes])
            inverse_down = 1.0 / (1.0 + rate_down + rows[pl.ds(j, 1), lanes])
            ratio_up = rate_up * inverse_up
            ratio_down = rate_down * inverse_down
            up = up * ratio_up
            down = down * ratio_down
            if inverse is not None:
                inverse[i, :HALF] = inverse_up
                inverse[j, HALF:] = inverse_down
                ratio[i, :HALF] = ratio_up
                ratio[j, HALF:] = ratio_down
            if unit is not None:
                unit[i, :HALF] = up
                unit[j, HALF:] = down
            return up, down

        ones = jnp.ones((HALF, LANES), F32)
        return jnp.concatenate(loop(X, one, (ones, ones)), axis=0)

    def weights(inverse, ratio, weight):
        def one(i, carry):
            up, down = carry
            j = X - 1 - i
            weight[j, :HALF] = inverse[j, :HALF] * up
            weight[i, HALF:] = inverse[i, HALF:] * down
            return up * ratio[j, :HALF], down * ratio[i, HALF:]

        ones = jnp.ones((HALF, LANES), F32)
        loop(X, one, (ones, ones))

    def sweep(s, h):
        def one(i, carry):
            up, down = carry
            j = X - 1 - i
            up = free[s, h, i, :HALF] * inverse[s, h, i, :HALF] + ratio[s, h, i, :HALF] * up
            down = free[s, h, j, HALF:] * inverse[s, h, j, HALF:] + ratio[s, h, j, HALF:] * down
            free[s, h, i, :HALF] = up
            free[s, h, j, HALF:] = down
            return up, down

        zeros = jnp.zeros((HALF, LANES), F32)
        return jnp.concatenate(loop(X, one, (zeros, zeros)), axis=0)

    wide = jnp.concatenate([absorb_now[0], absorb_now[1], jnp.zeros((LANES - 2 * X, 2 * LANES), F32)], axis=0)
    turned[...] = wide.T
    packed = turned[pl.ds(0, ROWS // 4, stride=4), :]
    for i in range(1, 4):
        packed = packed + pltpu.roll(turned[pl.ds(i, ROWS // 4, stride=4), :], 2 * X * i, axis=1)
    for o in range(CYCLE):
        send_absorb[o] = packed[2 * o : 2 * o + 2]

    for h in range(HALVES):
        for s in range(STEPS):
            coefficients(absorb_now.at[s], h, inverse.at[s, h], ratio.at[s, h], unit.at[s, h])
        weights(inverse.at[1, h], ratio.at[1, h], weight.at[h])
    gained = []
    for s in range(STEPS):
        gain = jnp.where(first[s], decay[0:1], decay[1:2])
        gained.append(column(gain) * modes[...])
        left_comp[s] = jnp.concatenate(split(gained[s].T), axis=1)
    left_mid[...] = left_operand(
        jnp.dot(ordin[...], gained[0], preferred_element_type=F32, precision=lax.Precision.HIGHEST)
    )
    left_out[...] = left_operand(gained[1])
    for h in range(HALVES):
        q_load[h].wait()

        def sources(i):
            value = jnp.concatenate(
                [q_in[h, pl.ds(2 * i, M, stride=X), :], q_in[h, pl.ds(2 * i + 1, M, stride=X), :]], axis=1
            )
            result = product(left_in[...], value)
            free[0, h, 2 * i] = result[:, :LANES]
            free[0, h, 2 * i + 1] = result[:, LANES:]

        loop(X // 2, sources)
        outflow = sweep(0, h)

        def sources_free(i, outflow):
            value = jnp.concatenate([free[0, h, 2 * i], free[0, h, 2 * i + 1]], axis=1)
            result = product(left_mid[...], value)
            return outflow + weight[h, 2 * i] * result[:, :LANES] + weight[h, 2 * i + 1] * result[:, LANES:]

        outflow_next = loop(X // 2, sources_free, jnp.zeros((M, LANES), F32))
        send_out[pl.ds(LANES * h, LANES)] = jnp.concatenate([outflow, outflow_next], axis=0).T

    def own_rows(p):
        return pl.ds(pl.multiple_of(OWN * p, OWN), OWN)

    def remote(source, target, send_sem, recv_sem, place, section):
        pltpu.make_async_remote_copy(
            src_ref=source,
            dst_ref=target,
            send_sem=send_sem,
            recv_sem=recv_sem,
            device_id={"gx": place, "col": section},
            device_id_type=pl.DeviceIdType.MESH,
        ).start()

    pl.semaphore_wait(barrier, CYCLE + SECTIONS - 2)
    for p in far_places():
        remote(send_absorb.at[p], recv_absorb.at[me], absorb_send, absorb_recv, p, col)
    for p in far_places():
        remote(send_out.at[own_rows(p)], recv_out.at[own_rows(me)], out_send, out_recv, p, col)
    recv_absorb[me] = send_absorb[me]
    recv_out[own_rows(me)] = send_out[own_rows(me)]

    comp_load.wait()
    for s in range(STEPS):
        for h in range(HALVES):

            def widen(i):
                rows = pl.ds(8 * X * i, 8 * X)
                comp_wide[s, h, rows] = comp[s, rows, pl.ds(LANES * h, LANES)].astype(F32)

            loop(M // 8, widen)

            def to_ordinates(i):
                value = jnp.concatenate(
                    [
                        comp_wide[s, h, pl.ds(2 * i, M, stride=X), :],
                        comp_wide[s, h, pl.ds(2 * i + 1, M, stride=X), :],
                    ],
                    axis=1,
                ).astype(BF16)
                result = jnp.dot(left_comp[s], jnp.concatenate([value, value], axis=0), preferred_element_type=F32)
                comp_ordin[s, h, 2 * i] = result[:, :LANES]
                comp_ordin[s, h, 2 * i + 1] = result[:, LANES:]

            loop(X // 2, to_ordinates)

    wait_for(recv_absorb.at[pl.ds(0, CYCLE - 1)], absorb_recv)
    for p in range(CYCLE):
        own_wide[pl.ds(2 * p, 2)] = recv_absorb[p]
    for h in range(HALVES):
        parts = [own_wide[...]] if h == 0 else [pltpu.roll(own_wide[...], LANES - 4 * X * h, axis=1)]
        parts.append(pltpu.roll(own_wide[...], LANES - 4 * X * h - 2 * X, axis=1))
        by_cell = jnp.concatenate(parts, axis=0).T
        for s in range(STEPS):
            own_absorb[s, :, pl.ds(LANES * h, LANES)] = by_cell[X * s : X * s + X]
    for h in range(HALVES):
        whole = [
            coefficients(own_absorb.at[0], h, None, None, own_unit.at[h]),
            coefficients(own_absorb.at[1], h, own_inverse.at[h], own_ratio.at[h], None),
        ]
        weights(own_inverse.at[h], own_ratio.at[h], own_weight.at[h])
        by_line = jnp.concatenate(whole, axis=0).T
        for i in range(2):
            own_factor[pl.ds(2 * h + i, M, stride=4), :] = by_line[M * i : M * i + M]

    lane = lax.broadcasted_iota(jnp.int32, (OWN, LANES), 1)
    upward = lax.rem(lane, M) < HALF
    ones, zeros = jnp.ones((OWN, LANES), F32), jnp.zeros((OWN, LANES), F32)

    def placed(ref, k):
        return jnp.where(upward, ref[OWN * k : OWN * k + OWN], ref[OWN * (CYCLE - 1 - k) : OWN * (CYCLE - k)])

    whole_unit = ones
    for k in range(CYCLE):
        prefix_unit[OWN * k : OWN * k + OWN] = whole_unit
        whole_unit = whole_unit * placed(own_factor, k)
    closing = 1.0 - whole_unit

    def solve(s, outflow):
        whole_free = zeros
        for k in range(CYCLE):
            prefix_free[OWN * k : OWN * k + OWN] = whole_free
            whole_free = placed(own_factor, k) * whole_free + outflow(k)
        entry = whole_free / closing
        for p in range(CYCLE):
            send_flow[s, OWN * p : OWN * p + OWN] = placed(prefix_unit, p) * entry + placed(prefix_free, p)
        for p in far_places():
            remote(
                send_flow.at[s, own_rows(p)], recv_flow.at[s, own_rows(me)], flow_send.at[s], flow_recv.at[s], p, col
            )
        recv_flow[s, own_rows(me)] = send_flow[s, own_rows(me)]

    wait_for(recv_out.at[pl.ds(0, ROWS - OWN)], out_recv)
    solve(0, lambda k: placed(recv_out, k))

    for h in range(HALVES):
        rows = [send_flow[0, pl.ds(2 * h + i, M, stride=4), :] for i in range(2)]
        inflow = jnp.concatenate(rows, axis=0).T[:M]

        def extra(i, outflow):
            value = jnp.concatenate([own_unit[h, 2 * i] * inflow, own_unit[h, 2 * i + 1] * inflow], axis=1)
            result = product(left_mid[...], value)
            return outflow + own_weight[h, 2 * i] * result[:, :LANES] + own_weight[h, 2 * i + 1] * result[:, LANES:]

        added = loop(X // 2, extra, jnp.zeros((M, LANES), F32))
        by_line = jnp.concatenate([jnp.zeros((M, LANES), F32), added], axis=0).T
        for i in range(2):
            own_extra[pl.ds(2 * h + i, M, stride=4), :] = by_line[M * i : M * i + M]
    solve(1, lambda k: placed(recv_out, k) + placed(own_extra, k))

    def inflows(s, h):
        return recv_flow[s, pl.ds(LANES * h, LANES)].T[M * s : M * s + M]

    def to_sections(source, target, send_sem, recv_sem):
        for section in far_sections():
            remote(source, target, send_sem, recv_sem, me, section)

    wait_for(recv_flow.at[0, pl.ds(0, ROWS - OWN)], flow_recv.at[0])
    for h in range(HALVES):
        inflow = inflows(0, h)

        def middle(i):
            solved = [free[0, h, 2 * i + j] + unit[0, h, 2 * i + j] * inflow for j in range(2)]
            for j in range(2):
                send_early[pl.ds(X * h + 2 * i + j, 1)] = jnp.sum(
                    solved[j] * comp_ordin[0, h, 2 * i + j], axis=0, keepdims=True
                )
            result = product(left_mid[...], jnp.concatenate(solved, axis=1))
            free[1, h, 2 * i] = result[:, :LANES]
            free[1, h, 2 * i + 1] = result[:, LANES:]

        loop(X // 2, middle)
    for s in range(STEPS):
        send_early[pl.ds(2 * X + 8 * s, 8)] = jnp.broadcast_to(labels[0, s].astype(F32), (8, LANES))
    to_sections(send_early, recv_early.at[col], early_send, early_recv)
    recv_early[col] = send_early[...]
    for h in range(HALVES):
        sweep(1, h)

    wait_for(recv_flow.at[1, pl.ds(0, ROWS - OWN)], flow_recv.at[1])
    for h in range(HALVES):
        inflow = inflows(1, h)

        def last_density(i):
            solved = free[1, h, i] + unit[1, h, i] * inflow
            free[1, h, i] = solved
            send_late[h, pl.ds(i, 1)] = jnp.sum(solved * comp_ordin[1, h, i], axis=0, keepdims=True)

        loop(X, last_density)
        to_sections(send_late.at[h], recv_late.at[h, col], late_send.at[h], late_recv.at[h])
        recv_late[h, col] = send_late[h]
    q_store = [
        pltpu.make_async_copy(q_out.at[h], out_ref.at[:, pl.ds(LANES * h, LANES)], store_sem.at[h])
        for h in range(HALVES)
    ]
    for h in range(HALVES):

        def last(i):
            value = jnp.concatenate([free[1, h, 2 * i], free[1, h, 2 * i + 1]], axis=1)
            result = product(left_out[...], value)
            q_out[h, pl.ds(2 * i, M, stride=X), :] = result[:, :LANES]
            q_out[h, pl.ds(2 * i + 1, M, stride=X), :] = result[:, LANES:]

        loop(X // 2, last)
        q_store[h].start()

    wait_for(recv_early.at[pl.ds(0, SECTIONS - 1)], early_recv)

    def add_densities(carry, terms, s):
        def one(c, carry):
            total_a, total_b = carry
            label = recv_early[c, pl.ds(2 * X + 8 * s, 8)]
            is_a = jnp.concatenate([label, label], axis=0) == 0.0
            term = terms(c)
            return total_a + jnp.where(is_a, term, 0.0), total_b + jnp.where(is_a, 0.0, term)

        return loop(SECTIONS, one, carry)

    none = jnp.zeros((X, LANES), F32)
    early = [add_densities((none, none), lambda c, h=h: recv_early[c, pl.ds(X * h, X)], 0) for h in range(HALVES)]
    for h in range(HALVES):
        wait_for(recv_late.at[h, pl.ds(0, SECTIONS - 1)], late_recv.at[h])
        total_a, total_b = add_densities(early[h], lambda c, h=h: recv_late[h, c], 1)
        dens_ref[0, :, pl.ds(LANES * h, LANES)] = total_a
        dens_ref[1, :, pl.ds(LANES * h, LANES)] = total_b

    wait_for(send_absorb.at[pl.ds(0, CYCLE - 1)], absorb_send)
    wait_for(send_out.at[pl.ds(0, ROWS - OWN)], out_send)
    for s in range(STEPS):
        wait_for(send_flow.at[s, pl.ds(0, ROWS - OWN)], flow_send.at[s])
    wait_for(recv_early.at[pl.ds(0, SECTIONS - 1)], early_send)
    for h in range(HALVES):
        wait_for(recv_late.at[h, pl.ds(0, SECTIONS - 1)], late_send.at[h])
    for copy in q_store:
        copy.wait()


def store(q_ref, dens_ref, q_out, dens_out, sem):
    part = M * X // STORES
    copies = [pltpu.make_async_copy(dens_ref, dens_out, sem.at[STORES])]
    for i in range(STORES):
        rows = pl.ds(part * i, part)
        copies.append(pltpu.make_async_copy(q_ref.at[rows], q_out.at[rows], sem.at[i]))
    for copy in copies:
        copy.start()
    for copy in copies:
        copy.wait()


def body(propagator, complement, labels, absorption, to_ordinates, to_modes, upwind, mode_decay):
    rows, lines = M * X, HALVES * LANES
    dma = pltpu.SemaphoreType.DMA
    anywhere = pl.BlockSpec(memory_space=pl.ANY)
    left = pltpu.VMEM((M, 3 * M), BF16)
    half_cells = pltpu.VMEM((HALVES, X, M, LANES), F32)
    cells = pltpu.VMEM((STEPS, HALVES, X, M, LANES), F32)
    by_line = pltpu.VMEM((ROWS, LANES), F32)
    flows = pltpu.VMEM((STEPS, ROWS, LANES), F32)
    pairs = pltpu.VMEM((CYCLE, 2, LANES), F32)
    scratch = [
        pltpu.VMEM((HALVES, rows, LANES), F32),
        pltpu.VMEM((HALVES, rows, LANES), F32),
        pltpu.VMEM((STEPS, rows, lines), BF16),
        pltpu.SMEM((1, STEPS), jnp.int32),
        pltpu.VMEM((2, X, lines), F32),
        pltpu.VMEM((M, M), F32),
        pltpu.VMEM((M, M), F32),
        pltpu.VMEM((1, M), F32),
        pltpu.VMEM((2, M), F32),
        pltpu.VMEM((M, LANES), F32),
        pltpu.VMEM((STEPS, X, lines), F32),
        left,
        left,
        left,
        pltpu.VMEM((STEPS, M, 2 * M), BF16),
        cells,
        cells,
        cells,
        cells,
        half_cells,
        pltpu.VMEM((STEPS, HALVES, rows, LANES), F32),
        cells,
        by_line,
        pairs,
        pairs,
        pltpu.VMEM((2 * CYCLE, LANES), F32),
        pltpu.VMEM((STEPS, X, lines), F32),
        half_cells,
        half_cells,
        half_cells,
        half_cells,
        by_line,
        by_line,
        by_line,
        by_line,
        by_line,
        by_line,
        flows,
        flows,
        pltpu.VMEM((3 * X, LANES), F32),
        pltpu.VMEM((SECTIONS, 3 * X, LANES), F32),
        pltpu.VMEM((HALVES, X, LANES), F32),
        pltpu.VMEM((HALVES, SECTIONS, X, LANES), F32),
        dma((6,)),
        dma((HALVES,)),
        dma,
        dma,
        dma,
        dma,
        dma,
        dma((STEPS,)),
        dma((STEPS,)),
        dma,
        dma,
        dma((HALVES,)),
        dma((HALVES,)),
        dma((HALVES,)),
    ]
    propagated, density = pl.pallas_call(
        kernel,
        out_shape=(
            jax.ShapeDtypeStruct((rows, lines), F32),
            jax.ShapeDtypeStruct((2, X, lines), F32),
        ),
        in_specs=[anywhere] * 8,
        out_specs=(anywhere, pl.BlockSpec(memory_space=pltpu.VMEM)),
        scratch_shapes=scratch,
        compiler_params=pltpu.CompilerParams(
            collective_id=0, has_side_effects=True, vmem_limit_bytes=48 * 1024 * 1024
        ),
        name="contour_steps",
    )(
        *(
            pltpu.with_memory_space_constraint(operand, pltpu.HBM)
            for operand in (
                propagator.reshape(rows, lines),
                complement.reshape(STEPS, rows, lines),
                labels,
                absorption,
                to_ordinates,
                to_modes,
                upwind.reshape(1, M),
                mode_decay,
            )
        )
    )
    propagated, density = pl.pallas_call(
        store,
        out_shape=(
            jax.ShapeDtypeStruct((rows, lines), F32),
            jax.ShapeDtypeStruct((2, X, lines), F32),
        ),
        in_specs=[anywhere] * 2,
        out_specs=(anywhere, anywhere),
        scratch_shapes=[dma((STORES + 1,))],
        compiler_params=pltpu.CompilerParams(vmem_limit_bytes=1024 * 1024),
        name="store_results",
    )(propagated, density)
    return propagated.reshape(1, M, X, lines), density


def solution(mesh):
    in_specs = (
        P("col", None, "gx", None),
        P("col", None, None, "gx", None),
        P("col", None),
        P(None, "gx", None),
        P(),
        P(),
        P(),
        P(),
    )
    out_specs = (P("col", None, "gx", None), P(None, "gx", None))
    return jax.shard_map(body, mesh=mesh, in_specs=in_specs, out_specs=out_specs, check_vma=False)
```

time: 40.5 us -> 32.8 us (0.81)
  Pallas kernels: 39.8 us -> 32 us
    pallas_call x1, Pallas kernels: 38.8 us -> 31 us  [body(): pl.pallas_call(kernel, out_shape=(jax.ShapeDtypeStruct((rows, lines), F32...]
where the time goes in v4:
time: 32.8 us; the launch traced here: 32.7 us
  Pallas kernels  32 us (98%)
  between operations  0.64 us (2%)
    pallas_call x1, Pallas kernels, body(): pl.pallas_call(kernel, out_shape=(jax.ShapeDtypeStruct((rows, lines), F32...  31 us
    pallas_call x1, Pallas kernels, body(): pl.pallas_call(store, out_shape=(jax.ShapeDtypeStruct((rows, lines), F32)...  1.02 us

profile of v4, /device:TPU:1, one launch (start us, length us, event | category | flops | bytes accessed | tf_op | source)
XLA Modules:
  0.0 32.7 jit_solution(9597260422457260193)
XLA Ops:
  0.6 31.0 %contour_steps.1 = (f32[1024,256]{1,0:T(8,128)S(1)}, f32[2,16,256]{2,1,0:T(8,128)S(1)}) custom-call(f32[1024,256]{1,0:T(8,128)} %bitcast.4, bf16[2,1024,256]{2,1,0:T(8,128)(2,1)} %bitcast.5, s32[1,2]{1,0:T(1,128)} %labels_ref.1, f32[2,16,256]{2,1,0:T(8,128)} %absorb_ref.1, f32[64,64]{1,0:T(8,128)} %ordin_ref.1, f32[64,64]{1,0:T(8,128)} %modes_ref.1, ...), custom_call_target="tpu_custom_call" | custom-call | tf_op jit(solution)/shard_map/contour_steps/pallas_call | solution.py:561
  31.7 1.0 %store_results.1 = (f32[1024,256]{1,0:T(8,128)}, f32[2,16,256]{2,1,0:T(8,128)}) custom-call(f32[1024,256]{1,0:T(8,128)S(1)} %get-tuple-element.6.q_ref, f32[2,16,256]{2,1,0:T(8,128)S(1)} %get-tuple-element.7.dens_ref), custom_call_target="tpu_custom_call" | custom-call | tf_op jit(solution)/shard_map/store_results/pallas_call | solution.py:589

commit v5 on v4

--- a/solution.py
+++ b/solution.py
@@ -13,8 +13,7 @@
 HALVES = 2
 STEPS = 2
 CYCLE, SECTIONS = 32, 8
-OWN = 8
-ROWS = CYCLE * OWN
+OWN = 4
 RING_Z, RING_Y, RING_X = 8, 4, 4
 FAR_Z, FAR_Y, FAR_X = (4, 3, 5, 2, 6, 1, 7, 0), (2, 1, 3, 0), (2, 1, 3, 0)
 STORES = 4
@@ -106,9 +105,11 @@
     own_factor,
     prefix_unit,
     prefix_free,
+    own_flow,
     own_extra,
     send_flow,
     recv_flow,
+    flow,
     send_early,
     recv_early,
     send_late,
@@ -240,11 +241,12 @@
 
     wide = jnp.concatenate([absorb_now[0], absorb_now[1], jnp.zeros((LANES - 2 * X, 2 * LANES), F32)], axis=0)
     turned[...] = wide.T
-    packed = turned[pl.ds(0, ROWS // 4, stride=4), :]
-    for i in range(1, 4):
-        packed = packed + pltpu.roll(turned[pl.ds(i, ROWS // 4, stride=4), :], 2 * X * i, axis=1)
-    for o in range(CYCLE):
-        send_absorb[o] = packed[2 * o : 2 * o + 2]
+    for h in range(HALVES):
+        packed = turned[pl.ds(LANES * h, CYCLE, stride=OWN), :]
+        for r in range(1, OWN):
+            packed = packed + pltpu.roll(turned[pl.ds(LANES * h + r, CYCLE, stride=OWN), :], 2 * X * r, axis=1)
+        for o in range(CYCLE):
+            send_absorb[o, h : h + 1] = packed[o : o + 1]
 
     for h in range(HALVES):
         for s in range(STEPS):
@@ -259,6 +261,7 @@
         jnp.dot(ordin[...], gained[0], preferred_element_type=F32, precision=lax.Precision.HIGHEST)
     )
     left_out[...] = left_operand(gained[1])
+    outflows = [[], []]
     for h in range(HALVES):
         q_load[h].wait()
 
@@ -271,18 +274,18 @@
             free[0, h, 2 * i + 1] = result[:, LANES:]
 
         loop(X // 2, sources)
-        outflow = sweep(0, h)
+        outflows[0].append(sweep(0, h))
 
         def sources_free(i, outflow):
             value = jnp.concatenate([free[0, h, 2 * i], free[0, h, 2 * i + 1]], axis=1)
             result = product(left_mid[...], value)
             return outflow + weight[h, 2 * i] * result[:, :LANES] + weight[h, 2 * i + 1] * result[:, LANES:]
 
-        outflow_next = loop(X // 2, sources_free, jnp.zeros((M, LANES), F32))
-        send_out[pl.ds(LANES * h, LANES)] = jnp.concatenate([outflow, outflow_next], axis=0).T
-
-    def own_rows(p):
-        return pl.ds(pl.multiple_of(OWN * p, OWN), OWN)
+        outflows[1].append(loop(X // 2, sources_free, jnp.zeros((M, LANES), F32)))
+    for s in range(STEPS):
+        by_line = jnp.concatenate(outflows[s], axis=0).T
+        for o in range(CYCLE):
+            send_out[s, o] = by_line[OWN * o : OWN * o + OWN]
 
     def remote(source, target, send_sem, recv_sem, place, section):
         pltpu.make_async_remote_copy(
@@ -298,9 +301,12 @@
     for p in far_places():
         remote(send_absorb.at[p], recv_absorb.at[me], absorb_send, absorb_recv, p, col)
     for p in far_places():
-        remote(send_out.at[own_rows(p)], recv_out.at[own_rows(me)], out_send, out_recv, p, col)
+        remote(send_out.at[0, p], recv_out.at[0, me], out_send.at[0], out_recv.at[0], p, col)
+    for p in far_places():
+        remote(send_out.at[1, p], recv_out.at[1, me], out_send.at[1], out_recv.at[1], p, col)
     recv_absorb[me] = send_absorb[me]
-    recv_out[own_rows(me)] = send_out[own_rows(me)]
+    for s in range(STEPS):
+        recv_out[s, me] = send_out[s, me]
 
     comp_load.wait()
     for s in range(STEPS):
@@ -327,79 +333,90 @@
             loop(X // 2, to_ordinates)
 
     wait_for(recv_absorb.at[pl.ds(0, CYCLE - 1)], absorb_recv)
-    for p in range(CYCLE):
-        own_wide[pl.ds(2 * p, 2)] = recv_absorb[p]
-    for h in range(HALVES):
-        parts = [own_wide[...]] if h == 0 else [pltpu.roll(own_wide[...], LANES - 4 * X * h, axis=1)]
-        parts.append(pltpu.roll(own_wide[...], LANES - 4 * X * h - 2 * X, axis=1))
-        by_cell = jnp.concatenate(parts, axis=0).T
+    for h in range(HALVES):
+        for p in range(CYCLE):
+            own_wide[p : p + 1] = recv_absorb[p, h : h + 1]
+        for r in range(OWN):
+            part = own_wide[...]
+            if r:
+                part = pltpu.roll(part, LANES - 2 * X * r, axis=1)
+            turned[pl.ds(LANES * h + r, CYCLE, stride=OWN), :] = part
+        by_cell = turned[pl.ds(LANES * h, LANES)].T
         for s in range(STEPS):
             own_absorb[s, :, pl.ds(LANES * h, LANES)] = by_cell[X * s : X * s + X]
-    for h in range(HALVES):
-        whole = [
-            coefficients(own_absorb.at[0], h, None, None, own_unit.at[h]),
-            coefficients(own_absorb.at[1], h, own_inverse.at[h], own_ratio.at[h], None),
-        ]
+    whole = [[], []]
+    for h in range(HALVES):
+        whole[0].append(coefficients(own_absorb.at[0], h, None, None, own_unit.at[h]))
+        whole[1].append(coefficients(own_absorb.at[1], h, own_inverse.at[h], own_ratio.at[h], None))
         weights(own_inverse.at[h], own_ratio.at[h], own_weight.at[h])
-        by_line = jnp.concatenate(whole, axis=0).T
-        for i in range(2):
-            own_factor[pl.ds(2 * h + i, M, stride=4), :] = by_line[M * i : M * i + M]
+    for s in range(STEPS):
+        own_factor[s] = jnp.concatenate(whole[s], axis=0).T
 
     lane = lax.broadcasted_iota(jnp.int32, (OWN, LANES), 1)
     upward = lax.rem(lane, M) < HALF
     ones, zeros = jnp.ones((OWN, LANES), F32), jnp.zeros((OWN, LANES), F32)
 
-    def placed(ref, k):
-        return jnp.where(upward, ref[OWN * k : OWN * k + OWN], ref[OWN * (CYCLE - 1 - k) : OWN * (CYCLE - k)])
-
-    whole_unit = ones
-    for k in range(CYCLE):
-        prefix_unit[OWN * k : OWN * k + OWN] = whole_unit
-        whole_unit = whole_unit * placed(own_factor, k)
-    closing = 1.0 - whole_unit
+    def placed(slab, k):
+        return jnp.where(upward, slab(k), slab(CYCLE - 1 - k))
+
+    def rows_of(ref):
+        return lambda k: ref[OWN * k : OWN * k + OWN]
+
+    closing = []
+    for s in range(STEPS):
+        whole_unit = ones
+        for k in range(CYCLE):
+            prefix_unit[s, OWN * k : OWN * k + OWN] = whole_unit
+            whole_unit = whole_unit * placed(rows_of(own_factor.at[s]), k)
+        closing.append(1.0 - whole_unit)
 
     def solve(s, outflow):
         whole_free = zeros
         for k in range(CYCLE):
             prefix_free[OWN * k : OWN * k + OWN] = whole_free
-            whole_free = placed(own_factor, k) * whole_free + outflow(k)
-        entry = whole_free / closing
+            whole_free = placed(rows_of(own_factor.at[s]), k) * whole_free + placed(outflow, k)
+        entry = whole_free / closing[s]
         for p in range(CYCLE):
-            send_flow[s, OWN * p : OWN * p + OWN] = placed(prefix_unit, p) * entry + placed(prefix_free, p)
+            inflow = placed(rows_of(prefix_unit.at[s]), p) * entry + placed(rows_of(prefix_free), p)
+            send_flow[s, p] = inflow
+            if s == 0:
+                own_flow[OWN * p : OWN * p + OWN] = inflow
         for p in far_places():
-            remote(
-                send_flow.at[s, own_rows(p)], recv_flow.at[s, own_rows(me)], flow_send.at[s], flow_recv.at[s], p, col
-            )
-        recv_flow[s, own_rows(me)] = send_flow[s, own_rows(me)]
-
-    wait_for(recv_out.at[pl.ds(0, ROWS - OWN)], out_recv)
-    solve(0, lambda k: placed(recv_out, k))
-
-    for h in range(HALVES):
-        rows = [send_flow[0, pl.ds(2 * h + i, M, stride=4), :] for i in range(2)]
-        inflow = jnp.concatenate(rows, axis=0).T[:M]
+            remote(send_flow.at[s, p], recv_flow.at[s, me], flow_send.at[s], flow_recv.at[s], p, col)
+        recv_flow[s, me] = send_flow[s, me]
+
+    wait_for(recv_out.at[0, pl.ds(0, CYCLE - 1)], out_recv.at[0])
+    solve(0, lambda p: recv_out[0, p])
+
+    own_inflow = own_flow[...].T
+    added = []
+    for h in range(HALVES):
+        inflow = own_inflow[M * h : M * h + M]
 
         def extra(i, outflow):
             value = jnp.concatenate([own_unit[h, 2 * i] * inflow, own_unit[h, 2 * i + 1] * inflow], axis=1)
             result = product(left_mid[...], value)
             return outflow + own_weight[h, 2 * i] * result[:, :LANES] + own_weight[h, 2 * i + 1] * result[:, LANES:]
 
-        added = loop(X // 2, extra, jnp.zeros((M, LANES), F32))
-        by_line = jnp.concatenate([jnp.zeros((M, LANES), F32), added], axis=0).T
-        for i in range(2):
-            own_extra[pl.ds(2 * h + i, M, stride=4), :] = by_line[M * i : M * i + M]
-    solve(1, lambda k: placed(recv_out, k) + placed(own_extra, k))
-
-    def inflows(s, h):
-        return recv_flow[s, pl.ds(LANES * h, LANES)].T[M * s : M * s + M]
+        added.append(loop(X // 2, extra, jnp.zeros((M, LANES), F32)))
+    own_extra[...] = jnp.concatenate(added, axis=0).T
+    wait_for(recv_out.at[1, pl.ds(0, CYCLE - 1)], out_recv.at[1])
+    solve(1, lambda p: recv_out[1, p] + rows_of(own_extra)(p))
+
+    def inflows(s):
+        wait_for(recv_flow.at[s, pl.ds(0, CYCLE - 1)], flow_recv.at[s])
+        for o in range(CYCLE):
+            flow[OWN * o : OWN * o + OWN] = recv_flow[s, o]
+        both = flow[...].T
+        return [both[M * h : M * h + M] for h in range(HALVES)]
 
     def to_sections(source, target, send_sem, recv_sem):
         for section in far_sections():
             remote(source, target, send_sem, recv_sem, me, section)
 
-    wait_for(recv_flow.at[0, pl.ds(0, ROWS - OWN)], flow_recv.at[0])
-    for h in range(HALVES):
-        inflow = inflows(0, h)
+    inflow_first = inflows(0)
+    for h in range(HALVES):
+        inflow = inflow_first[h]
 
         def middle(i):
             solved = [free[0, h, 2 * i + j] + unit[0, h, 2 * i + j] * inflow for j in range(2)]
@@ -419,9 +436,9 @@
     for h in range(HALVES):
         sweep(1, h)
 
-    wait_for(recv_flow.at[1, pl.ds(0, ROWS - OWN)], flow_recv.at[1])
-    for h in range(HALVES):
-        inflow = inflows(1, h)
+    inflow_second = inflows(1)
+    for h in range(HALVES):
+        inflow = inflow_second[h]
 
         def last_density(i):
             solved = free[1, h, i] + unit[1, h, i] * inflow
@@ -467,9 +484,9 @@
         dens_ref[1, :, pl.ds(LANES * h, LANES)] = total_b
 
     wait_for(send_absorb.at[pl.ds(0, CYCLE - 1)], absorb_send)
-    wait_for(send_out.at[pl.ds(0, ROWS - OWN)], out_send)
-    for s in range(STEPS):
-        wait_for(send_flow.at[s, pl.ds(0, ROWS - OWN)], flow_send.at[s])
+    for s in range(STEPS):
+        wait_for(send_out.at[s, pl.ds(0, CYCLE - 1)], out_send.at[s])
+        wait_for(send_flow.at[s, pl.ds(0, CYCLE - 1)], flow_send.at[s])
     wait_for(recv_early.at[pl.ds(0, SECTIONS - 1)], early_send)
     for h in range(HALVES):
         wait_for(recv_late.at[h, pl.ds(0, SECTIONS - 1)], late_send.at[h])
@@ -496,8 +513,9 @@
     left = pltpu.VMEM((M, 3 * M), BF16)
     half_cells = pltpu.VMEM((HALVES, X, M, LANES), F32)
     cells = pltpu.VMEM((STEPS, HALVES, X, M, LANES), F32)
-    by_line = pltpu.VMEM((ROWS, LANES), F32)
-    flows = pltpu.VMEM((STEPS, ROWS, LANES), F32)
+    by_line = pltpu.VMEM((LANES, LANES), F32)
+    both_by_line = pltpu.VMEM((STEPS, LANES, LANES), F32)
+    flows = pltpu.VMEM((STEPS, CYCLE, OWN, LANES), F32)
     pairs = pltpu.VMEM((CYCLE, 2, LANES), F32)
     scratch = [
         pltpu.VMEM((HALVES, rows, LANES), F32),
@@ -522,23 +540,25 @@
         half_cells,
         pltpu.VMEM((STEPS, HALVES, rows, LANES), F32),
         cells,
-        by_line,
+        pltpu.VMEM((HALVES * LANES, LANES), F32),
         pairs,
         pairs,
-        pltpu.VMEM((2 * CYCLE, LANES), F32),
+        pltpu.VMEM((CYCLE, LANES), F32),
         pltpu.VMEM((STEPS, X, lines), F32),
         half_cells,
         half_cells,
         half_cells,
         half_cells,
-        by_line,
-        by_line,
-        by_line,
+        flows,
+        flows,
+        both_by_line,
+        both_by_line,
         by_line,
         by_line,
         by_line,
         flows,
         flows,
+        by_line,
         pltpu.VMEM((3 * X, LANES), F32),
         pltpu.VMEM((SECTIONS, 3 * X, LANES), F32),
         pltpu.VMEM((HALVES, X, LANES), F32),
@@ -548,8 +568,8 @@
         dma,
         dma,
         dma,
-        dma,
-        dma,
+        dma((STEPS,)),
+        dma((STEPS,)),
         dma((STEPS,)),
         dma((STEPS,)),
         dma,

time: 32.8 us -> 32.1 us (0.979)
  Pallas kernels: 32 us -> 31.3 us
    pallas_call x1, Pallas kernels: 31 us -> 30.3 us  [body(): pl.pallas_call(kernel, out_shape=(jax.ShapeDtypeStruct((rows, lines), F32...]
where the time goes in v5:
time: 32.1 us; the launch traced here: 32 us
  Pallas kernels  31.3 us (98%)
  between operations  0.64 us (2%)
    pallas_call x1, Pallas kernels, body(): pl.pallas_call(kernel, out_shape=(jax.ShapeDtypeStruct((rows, lines), F32...  30.3 us
    pallas_call x1, Pallas kernels, body(): pl.pallas_call(store, out_shape=(jax.ShapeDtypeStruct((rows, lines), F32)...  1.02 us

profile of v5, /device:TPU:1, one launch (start us, length us, event | category | flops | bytes accessed | tf_op | source)
XLA Modules:
  0.0 32.0 jit_solution(5175266934997816382)
XLA Ops:
  0.6 30.3 %contour_steps.1 = (f32[1024,256]{1,0:T(8,128)S(1)}, f32[2,16,256]{2,1,0:T(8,128)S(1)}) custom-call(f32[1024,256]{1,0:T(8,128)} %bitcast.4, bf16[2,1024,256]{2,1,0:T(8,128)(2,1)} %bitcast.5, s32[1,2]{1,0:T(1,128)} %labels_ref.1, f32[2,16,256]{2,1,0:T(8,128)} %absorb_ref.1, f32[64,64]{1,0:T(8,128)} %ordin_ref.1, f32[64,64]{1,0:T(8,128)} %modes_ref.1, ...), custom_call_target="tpu_custom_call" | custom-call | tf_op jit(solution)/shard_map/contour_steps/pallas_call | solution.py:581
  30.9 1.0 %store_results.1 = (f32[1024,256]{1,0:T(8,128)}, f32[2,16,256]{2,1,0:T(8,128)}) custom-call(f32[1024,256]{1,0:T(8,128)S(1)} %get-tuple-element.6.q_ref, f32[2,16,256]{2,1,0:T(8,128)S(1)} %get-tuple-element.7.dens_ref), custom_call_target="tpu_custom_call" | custom-call | tf_op jit(solution)/shard_map/store_results/pallas_call | solution.py:609

commit v6 on v5

--- a/solution.py
+++ b/solution.py
@@ -13,10 +13,12 @@
 HALVES = 2
 STEPS = 2
 CYCLE, SECTIONS = 32, 8
-OWN = 4
+OWN = 8
+OWNERS = LANES // OWN
+BLOCKS = 2
 RING_Z, RING_Y, RING_X = 8, 4, 4
 FAR_Z, FAR_Y, FAR_X = (4, 3, 5, 2, 6, 1, 7, 0), (2, 1, 3, 0), (2, 1, 3, 0)
-STORES = 4
+STORES = 2
 
 
 def loop(count, step, carry=None):
@@ -84,6 +86,8 @@
     left_mid,
     left_out,
     left_comp,
+    mids,
+    left_own,
     inverse,
     ratio,
     unit,
@@ -94,7 +98,7 @@
     turned,
     send_absorb,
     recv_absorb,
-    own_wide,
+    wide_rows,
     own_absorb,
     own_inverse,
     own_ratio,
@@ -109,7 +113,8 @@
     own_extra,
     send_flow,
     recv_flow,
-    flow,
+    send_label,
+    recv_label,
     send_early,
     recv_early,
     send_late,
@@ -123,6 +128,8 @@
     out_recv,
     flow_send,
     flow_recv,
+    label_send,
+    label_recv,
     early_send,
     early_recv,
     late_send,
@@ -133,12 +140,24 @@
     col = lax.axis_index("col")
     core = lax.rem(col, 2)
     my_z, my_y, my_x = me // RING_Y, lax.rem(me, RING_Y), col // 2
+    is_owner = core == 1
+    parity = lax.rem(my_z + my_y, 2)
+    owns_here = jnp.logical_and(is_owner, parity == 1)
+    owns_other = jnp.logical_and(is_owner, parity == 0)
+    my_owner = 2 * my_z + my_y // 2
+    owner_col = col - core + 1
+    served_col = col - 1 + parity
 
     def far_places():
         for dz in FAR_Z:
             for dy in FAR_Y:
-                if (dz, dy) != (0, 0):
-                    yield RING_Y * lax.rem(my_z + dz, RING_Z) + lax.rem(my_y + dy, RING_Y)
+                yield RING_Y * lax.rem(my_z + dz, RING_Z) + lax.rem(my_y + dy, RING_Y), (dz, dy) == (0, 0)
+
+    def far_owners():
+        for dz in FAR_Z:
+            for dh in (1, 0):
+                z, h = lax.rem(my_z + dz, RING_Z), lax.rem(my_y // 2 + dh, 2)
+                yield 2 * z + h, RING_Y * z + 2 * h + lax.rem(z + core, 2), (dz, dh) == (0, 0)
 
     def far_sections():
         for dx in FAR_X:
@@ -153,10 +172,25 @@
             barrier, inc=1, device_id={"gx": place, "col": section}, device_id_type=pl.DeviceIdType.MESH
         )
 
-    for place in far_places():
-        greet(place, col)
+    @pl.when(owns_here)
+    def _():
+        for place, here in far_places():
+            if not here:
+                greet(place, col)
+
+    @pl.when(owns_other)
+    def _():
+        for place, here in far_places():
+            greet(place, served_col)
+
+    @pl.when(jnp.logical_not(owns_here))
+    def _():
+        for o, place, near in far_owners():
+            greet(place, owner_col)
+
     for section in far_sections():
         greet(me, section)
+    greeted = jnp.where(owns_here, CYCLE - 1, jnp.where(owns_other, CYCLE + OWNERS, OWNERS)) + SECTIONS - 1
 
     small = [
         pltpu.make_async_copy(src, dst, load_sem.at[i])
@@ -242,11 +276,14 @@
     wide = jnp.concatenate([absorb_now[0], absorb_now[1], jnp.zeros((LANES - 2 * X, 2 * LANES), F32)], axis=0)
     turned[...] = wide.T
     for h in range(HALVES):
-        packed = turned[pl.ds(LANES * h, CYCLE, stride=OWN), :]
-        for r in range(1, OWN):
-            packed = packed + pltpu.roll(turned[pl.ds(LANES * h + r, CYCLE, stride=OWN), :], 2 * X * r, axis=1)
-        for o in range(CYCLE):
-            send_absorb[o, h : h + 1] = packed[o : o + 1]
+        for j in range(2):
+            base = LANES * h + 4 * j
+            packed = turned[pl.ds(base, OWNERS, stride=OWN), :]
+            for i in range(1, 4):
+                packed = packed + pltpu.roll(turned[pl.ds(base + i, OWNERS, stride=OWN), :], 2 * X * i, axis=1)
+            wide_rows[pl.ds(2 * h + j, OWNERS, stride=4), :] = packed
+    for o in range(OWNERS):
+        send_absorb[o] = wide_rows[4 * o : 4 * o + 4]
 
     for h in range(HALVES):
         for s in range(STEPS):
@@ -257,9 +294,15 @@
         gain = jnp.where(first[s], decay[0:1], decay[1:2])
         gained.append(column(gain) * modes[...])
         left_comp[s] = jnp.concatenate(split(gained[s].T), axis=1)
-    left_mid[...] = left_operand(
-        jnp.dot(ordin[...], gained[0], preferred_element_type=F32, precision=lax.Precision.HIGHEST)
-    )
+    for species in range(2):
+        mids[species] = jnp.dot(
+            ordin[...],
+            column(decay[species : species + 1]) * modes[...],
+            preferred_element_type=F32,
+            precision=lax.Precision.HIGHEST,
+        )
+    left_mid[...] = left_operand(jnp.where(first[0], mids[0], mids[1]))
+    send_label[...] = jnp.broadcast_to(labels[0, 0].astype(F32), (8, LANES))
     left_out[...] = left_operand(gained[1])
     outflows = [[], []]
     for h in range(HALVES):
@@ -283,9 +326,7 @@
 
         outflows[1].append(loop(X // 2, sources_free, jnp.zeros((M, LANES), F32)))
     for s in range(STEPS):
-        by_line = jnp.concatenate(outflows[s], axis=0).T
-        for o in range(CYCLE):
-            send_out[s, o] = by_line[OWN * o : OWN * o + OWN]
+        send_out[s] = jnp.concatenate(outflows[s], axis=0).T.reshape(OWNERS, OWN, LANES)
 
     def remote(source, target, send_sem, recv_sem, place, section):
         pltpu.make_async_remote_copy(
@@ -297,16 +338,53 @@
             device_id_type=pl.DeviceIdType.MESH,
         ).start()
 
-    pl.semaphore_wait(barrier, CYCLE + SECTIONS - 2)
-    for p in far_places():
-        remote(send_absorb.at[p], recv_absorb.at[me], absorb_send, absorb_recv, p, col)
-    for p in far_places():
-        remote(send_out.at[0, p], recv_out.at[0, me], out_send.at[0], out_recv.at[0], p, col)
-    for p in far_places():
-        remote(send_out.at[1, p], recv_out.at[1, me], out_send.at[1], out_recv.at[1], p, col)
-    recv_absorb[me] = send_absorb[me]
+    def to_owners(source, target, send_sem, recv_sem):
+        for o, place, near in far_owners():
+
+            def send(o=o, place=place):
+                remote(source.at[o], target.at[me], send_sem, recv_sem, place, owner_col)
+
+            if near:
+                pl.when(jnp.logical_not(owns_here))(send)
+            else:
+                send()
+
+        @pl.when(owns_here)
+        def _():
+            target[me] = source[my_owner]
+
+    def wait_for_slabs(ref, sem):
+        @pl.when(owns_here)
+        def _():
+            wait_for(ref.at[pl.ds(0, CYCLE - 1)], sem)
+
+        @pl.when(owns_other)
+        def _():
+            wait_for(ref, sem)
+
+    def wait_for_owners(ref, sem):
+        @pl.when(owns_here)
+        def _():
+            wait_for(ref.at[pl.ds(0, OWNERS - 1)], sem)
+
+        @pl.when(jnp.logical_not(owns_here))
+        def _():
+            wait_for(ref, sem)
+
+    pl.semaphore_wait(barrier, greeted)
+    tells = jnp.logical_and(core == 0, parity == 0)
+
+    @pl.when(tells)
+    def _():
+        remote(send_label, recv_label, label_send, label_recv, me, owner_col)
+
+    @pl.when(owns_here)
+    def _():
+        recv_label[...] = send_label[...]
+
+    to_owners(send_absorb, recv_absorb, absorb_send, absorb_recv)
     for s in range(STEPS):
-        recv_out[s, me] = send_out[s, me]
+        to_owners(send_out.at[s], recv_out.at[s], out_send.at[s], out_recv.at[s])
 
     comp_load.wait()
     for s in range(STEPS):
@@ -332,82 +410,109 @@
 
             loop(X // 2, to_ordinates)
 
-    wait_for(recv_absorb.at[pl.ds(0, CYCLE - 1)], absorb_recv)
-    for h in range(HALVES):
+    @pl.when(is_owner)
+    def _():
+        @pl.when(owns_other)
+        def _():
+            wait_for(recv_label, label_recv)
+
+        first_own = jnp.broadcast_to(recv_label[0:1, :M], (M, M)) == 0.0
+        left_own[...] = left_operand(jnp.where(first_own, mids[0], mids[1]))
+
+        wait_for_slabs(recv_absorb, absorb_recv)
         for p in range(CYCLE):
-            own_wide[p : p + 1] = recv_absorb[p, h : h + 1]
-        for r in range(OWN):
-            part = own_wide[...]
-            if r:
-                part = pltpu.roll(part, LANES - 2 * X * r, axis=1)
-            turned[pl.ds(LANES * h + r, CYCLE, stride=OWN), :] = part
-        by_cell = turned[pl.ds(LANES * h, LANES)].T
+            wide_rows[4 * p : 4 * p + 4] = recv_absorb[p]
+        blocks = [(h, g) for h in range(HALVES) for g in range(BLOCKS)]
+        for b, (h, g) in enumerate(blocks):
+            for j in range(2):
+                part = wide_rows[pl.ds(4 * OWNERS * g + 2 * h + j, OWNERS, stride=4), :]
+                for i in range(4):
+                    rolled = pltpu.roll(part, LANES - 2 * X * i, axis=1) if i else part
+                    turned[pl.ds(LANES * (b % 2) + 4 * j + i, OWNERS, stride=OWN), :] = rolled
+            by_cell = turned[pl.ds(LANES * (b % 2), LANES)].T
+            for s in range(STEPS):
+                own_absorb[s, :, pl.ds(LANES * b, LANES)] = by_cell[X * s : X * s + X]
+        whole = [{}, {}]
+        for b, block in enumerate(blocks):
+            whole[0][block] = coefficients(own_absorb.at[0], b, None, None, own_unit.at[b])
+            whole[1][block] = coefficients(own_absorb.at[1], b, own_inverse.at[b], own_ratio.at[b], None)
+            weights(own_inverse.at[b], own_ratio.at[b], own_weight.at[b])
         for s in range(STEPS):
-            own_absorb[s, :, pl.ds(LANES * h, LANES)] = by_cell[X * s : X * s + X]
-    whole = [[], []]
-    for h in range(HALVES):
-        whole[0].append(coefficients(own_absorb.at[0], h, None, None, own_unit.at[h]))
-        whole[1].append(coefficients(own_absorb.at[1], h, own_inverse.at[h], own_ratio.at[h], None))
-        weights(own_inverse.at[h], own_ratio.at[h], own_weight.at[h])
-    for s in range(STEPS):
-        own_factor[s] = jnp.concatenate(whole[s], axis=0).T
-
-    lane = lax.broadcasted_iota(jnp.int32, (OWN, LANES), 1)
-    upward = lax.rem(lane, M) < HALF
-    ones, zeros = jnp.ones((OWN, LANES), F32), jnp.zeros((OWN, LANES), F32)
-
-    def placed(slab, k):
-        return jnp.where(upward, slab(k), slab(CYCLE - 1 - k))
-
-    def rows_of(ref):
-        return lambda k: ref[OWN * k : OWN * k + OWN]
-
-    closing = []
-    for s in range(STEPS):
-        whole_unit = ones
-        for k in range(CYCLE):
-            prefix_unit[s, OWN * k : OWN * k + OWN] = whole_unit
-            whole_unit = whole_unit * placed(rows_of(own_factor.at[s]), k)
-        closing.append(1.0 - whole_unit)
-
-    def solve(s, outflow):
-        whole_free = zeros
-        for k in range(CYCLE):
-            prefix_free[OWN * k : OWN * k + OWN] = whole_free
-            whole_free = placed(rows_of(own_factor.at[s]), k) * whole_free + placed(outflow, k)
-        entry = whole_free / closing[s]
-        for p in range(CYCLE):
-            inflow = placed(rows_of(prefix_unit.at[s]), p) * entry + placed(rows_of(prefix_free), p)
-            send_flow[s, p] = inflow
-            if s == 0:
-                own_flow[OWN * p : OWN * p + OWN] = inflow
-        for p in far_places():
-            remote(send_flow.at[s, p], recv_flow.at[s, me], flow_send.at[s], flow_recv.at[s], p, col)
-        recv_flow[s, me] = send_flow[s, me]
-
-    wait_for(recv_out.at[0, pl.ds(0, CYCLE - 1)], out_recv.at[0])
-    solve(0, lambda p: recv_out[0, p])
-
-    own_inflow = own_flow[...].T
-    added = []
-    for h in range(HALVES):
-        inflow = own_inflow[M * h : M * h + M]
-
-        def extra(i, outflow):
-            value = jnp.concatenate([own_unit[h, 2 * i] * inflow, own_unit[h, 2 * i + 1] * inflow], axis=1)
-            result = product(left_mid[...], value)
-            return outflow + own_weight[h, 2 * i] * result[:, :LANES] + own_weight[h, 2 * i + 1] * result[:, LANES:]
-
-        added.append(loop(X // 2, extra, jnp.zeros((M, LANES), F32)))
-    own_extra[...] = jnp.concatenate(added, axis=0).T
-    wait_for(recv_out.at[1, pl.ds(0, CYCLE - 1)], out_recv.at[1])
-    solve(1, lambda p: recv_out[1, p] + rows_of(own_extra)(p))
+            for g in range(BLOCKS):
+                own_factor[s, pl.ds(LANES * g, LANES)] = jnp.concatenate(
+                    [whole[s][h, g] for h in range(HALVES)], axis=0
+                ).T
+
+        lane = lax.broadcasted_iota(jnp.int32, (OWN, LANES), 1)
+        upward = lax.rem(lane, M) < HALF
+        ones, zeros = jnp.ones((OWN, LANES), F32), jnp.zeros((OWN, LANES), F32)
+
+        def placed(slab, k):
+            return jnp.where(upward, slab(k), slab(CYCLE - 1 - k))
+
+        def rows_of(ref):
+            return lambda k: ref[OWN * k : OWN * k + OWN]
+
+        closing = []
+        for s in range(STEPS):
+            whole_unit = ones
+            for k in range(CYCLE):
+                prefix_unit[s, OWN * k : OWN * k + OWN] = whole_unit
+                whole_unit = whole_unit * placed(rows_of(own_factor.at[s]), k)
+            closing.append(1.0 - whole_unit)
+
+        def solve(s, outflow):
+            whole_free = zeros
+            for k in range(CYCLE):
+                prefix_free[OWN * k : OWN * k + OWN] = whole_free
+                whole_free = placed(rows_of(own_factor.at[s]), k) * whole_free + placed(outflow, k)
+            entry = whole_free / closing[s]
+            for p in range(CYCLE):
+                inflow = placed(rows_of(prefix_unit.at[s]), p) * entry + placed(rows_of(prefix_free), p)
+                send_flow[s, p] = inflow
+                if s == 0:
+                    own_flow[OWN * p : OWN * p + OWN] = inflow
+            for p, here in far_places():
+
+                def send(p=p):
+                    remote(
+                        send_flow.at[s, p], recv_flow.at[s, my_owner], flow_send.at[s], flow_recv.at[s], p, served_col
+                    )
+
+                if here:
+                    pl.when(owns_other)(send)
+                else:
+                    send()
+
+            @pl.when(owns_here)
+            def _():
+                recv_flow[s, my_owner] = send_flow[s, me]
+
+        wait_for_slabs(recv_out.at[0], out_recv.at[0])
+        solve(0, lambda p: recv_out[0, p])
+
+        added = {}
+        for g in range(BLOCKS):
+            own_inflow = own_flow[pl.ds(LANES * g, LANES)].T
+            for h in range(HALVES):
+                b = BLOCKS * h + g
+                inflow = own_inflow[M * h : M * h + M]
+
+                def extra(i, outflow):
+                    value = jnp.concatenate([own_unit[b, 2 * i] * inflow, own_unit[b, 2 * i + 1] * inflow], axis=1)
+                    result = product(left_own[...], value)
+                    return (
+                        outflow + own_weight[b, 2 * i] * result[:, :LANES] + own_weight[b, 2 * i + 1] * result[:, LANES:]
+                    )
+
+                added[h] = loop(X // 2, extra, jnp.zeros((M, LANES), F32))
+            own_extra[pl.ds(LANES * g, LANES)] = jnp.concatenate([added[h] for h in range(HALVES)], axis=0).T
+        wait_for_slabs(recv_out.at[1], out_recv.at[1])
+        solve(1, lambda p: recv_out[1, p] + rows_of(own_extra)(p))
 
     def inflows(s):
-        wait_for(recv_flow.at[s, pl.ds(0, CYCLE - 1)], flow_recv.at[s])
-        for o in range(CYCLE):
-            flow[OWN * o : OWN * o + OWN] = recv_flow[s, o]
-        both = flow[...].T
+        wait_for_owners(recv_flow.at[s], flow_recv.at[s])
+        both = recv_flow[s].reshape(LANES, LANES).T
         return [both[M * h : M * h + M] for h in range(HALVES)]
 
     def to_sections(source, target, send_sem, recv_sem):
@@ -483,10 +588,14 @@
         dens_ref[0, :, pl.ds(LANES * h, LANES)] = total_a
         dens_ref[1, :, pl.ds(LANES * h, LANES)] = total_b
 
-    wait_for(send_absorb.at[pl.ds(0, CYCLE - 1)], absorb_send)
+    @pl.when(tells)
+    def _():
+        wait_for(send_label, label_send)
+
+    wait_for_owners(send_absorb, absorb_send)
     for s in range(STEPS):
-        wait_for(send_out.at[s, pl.ds(0, CYCLE - 1)], out_send.at[s])
-        wait_for(send_flow.at[s, pl.ds(0, CYCLE - 1)], flow_send.at[s])
+        wait_for_owners(send_out.at[s], out_send.at[s])
+        wait_for_slabs(send_flow.at[s], flow_send.at[s])
     wait_for(recv_early.at[pl.ds(0, SECTIONS - 1)], early_send)
     for h in range(HALVES):
         wait_for(recv_late.at[h, pl.ds(0, SECTIONS - 1)], late_send.at[h])
@@ -513,10 +622,11 @@
     left = pltpu.VMEM((M, 3 * M), BF16)
     half_cells = pltpu.VMEM((HALVES, X, M, LANES), F32)
     cells = pltpu.VMEM((STEPS, HALVES, X, M, LANES), F32)
-    by_line = pltpu.VMEM((LANES, LANES), F32)
-    both_by_line = pltpu.VMEM((STEPS, LANES, LANES), F32)
-    flows = pltpu.VMEM((STEPS, CYCLE, OWN, LANES), F32)
-    pairs = pltpu.VMEM((CYCLE, 2, LANES), F32)
+    own_cells = pltpu.VMEM((HALVES * BLOCKS, X, M, LANES), F32)
+    by_line = pltpu.VMEM((CYCLE * OWN, LANES), F32)
+    both_by_line = pltpu.VMEM((STEPS, CYCLE * OWN, LANES), F32)
+    by_owner = pltpu.VMEM((STEPS, OWNERS, OWN, LANES), F32)
+    by_slab = pltpu.VMEM((STEPS, CYCLE, OWN, LANES), F32)
     scratch = [
         pltpu.VMEM((HALVES, rows, LANES), F32),
         pltpu.VMEM((HALVES, rows, LANES), F32),
@@ -533,6 +643,8 @@
         left,
         left,
         pltpu.VMEM((STEPS, M, 2 * M), BF16),
+        pltpu.VMEM((2, M, M), F32),
+        left,
         cells,
         cells,
         cells,
@@ -541,24 +653,25 @@
         pltpu.VMEM((STEPS, HALVES, rows, LANES), F32),
         cells,
         pltpu.VMEM((HALVES * LANES, LANES), F32),
-        pairs,
-        pairs,
-        pltpu.VMEM((CYCLE, LANES), F32),
-        pltpu.VMEM((STEPS, X, lines), F32),
-        half_cells,
-        half_cells,
-        half_cells,
-        half_cells,
-        flows,
-        flows,
+        pltpu.VMEM((OWNERS, 4, LANES), F32),
+        pltpu.VMEM((CYCLE, 4, LANES), F32),
+        pltpu.VMEM((4 * CYCLE, LANES), F32),
+        pltpu.VMEM((STEPS, X, BLOCKS * lines), F32),
+        own_cells,
+        own_cells,
+        own_cells,
+        own_cells,
+        by_owner,
+        by_slab,
         both_by_line,
         both_by_line,
         by_line,
         by_line,
         by_line,
-        flows,
-        flows,
-        by_line,
+        by_slab,
+        by_owner,
+        pltpu.VMEM((8, LANES), F32),
+        pltpu.VMEM((8, LANES), F32),
         pltpu.VMEM((3 * X, LANES), F32),
         pltpu.VMEM((SECTIONS, 3 * X, LANES), F32),
         pltpu.VMEM((HALVES, X, LANES), F32),
@@ -572,6 +685,8 @@
         dma((STEPS,)),
         dma((STEPS,)),
         dma((STEPS,)),
+        dma,
+        dma,
         dma,
         dma,
         dma((HALVES,)),

time: 32.1 us -> 31.7 us (0.988)
  no operation moved by 1% of the time
where the time goes in v6:
time: 31.7 us; the launch traced here: 31.6 us
  Pallas kernels  31 us (98%)
  between operations  0.64 us (2%)
    pallas_call x1, Pallas kernels, body(): pl.pallas_call(kernel, out_shape=(jax.ShapeDtypeStruct((rows, lines), F32...  30 us
    pallas_call x1, Pallas kernels, body(): pl.pallas_call(store, out_shape=(jax.ShapeDtypeStruct((rows, lines), F32)...  1 us

profile of v6, /device:TPU:1, one launch (start us, length us, event | category | flops | bytes accessed | tf_op | source)
XLA Modules:
  0.0 31.6 jit_solution(2752312451088982908)
XLA Ops:
  0.6 30.0 %contour_steps.1 = (f32[1024,256]{1,0:T(8,128)S(1)}, f32[2,16,256]{2,1,0:T(8,128)S(1)}) custom-call(f32[1024,256]{1,0:T(8,128)} %bitcast.4, bf16[2,1024,256]{2,1,0:T(8,128)(2,1)} %bitcast.5, s32[1,2]{1,0:T(1,128)} %labels_ref.1, f32[2,16,256]{2,1,0:T(8,128)} %absorb_ref.1, f32[64,64]{1,0:T(8,128)} %ordin_ref.1, f32[64,64]{1,0:T(8,128)} %modes_ref.1, ...), custom_call_target="tpu_custom_call" | custom-call | tf_op jit(solution)/shard_map/contour_steps/pallas_call | solution.py:696
  30.6 1.0 %store_results.1 = (f32[1024,256]{1,0:T(8,128)}, f32[2,16,256]{2,1,0:T(8,128)}) custom-call(f32[1024,256]{1,0:T(8,128)S(1)} %get-tuple-element.6.q_ref, f32[2,16,256]{2,1,0:T(8,128)S(1)} %get-tuple-element.7.dens_ref), custom_call_target="tpu_custom_call" | custom-call | tf_op jit(solution)/shard_map/store_results/pallas_call | solution.py:724

commit v7 on v6

--- a/solution.py
+++ b/solution.py
@@ -302,7 +302,9 @@
             precision=lax.Precision.HIGHEST,
         )
     left_mid[...] = left_operand(jnp.where(first[0], mids[0], mids[1]))
-    send_label[...] = jnp.broadcast_to(labels[0, 0].astype(F32), (8, LANES))
+    for s in range(STEPS):
+        send_label[s : s + 1] = jnp.broadcast_to(labels[0, s].astype(F32), (1, LANES))
+    send_label[STEPS:] = jnp.zeros((8 - STEPS, LANES), F32)
     left_out[...] = left_operand(gained[1])
     outflows = [[], []]
     for h in range(HALVES):
@@ -372,19 +374,16 @@
             wait_for(ref, sem)
 
     pl.semaphore_wait(barrier, greeted)
-    tells = jnp.logical_and(core == 0, parity == 0)
-
-    @pl.when(tells)
-    def _():
-        remote(send_label, recv_label, label_send, label_recv, me, owner_col)
-
-    @pl.when(owns_here)
-    def _():
-        recv_label[...] = send_label[...]
-
     to_owners(send_absorb, recv_absorb, absorb_send, absorb_recv)
     for s in range(STEPS):
         to_owners(send_out.at[s], recv_out.at[s], out_send.at[s], out_recv.at[s])
+
+    def to_sections(source, target, send_sem, recv_sem):
+        for section in far_sections():
+            remote(source, target, send_sem, recv_sem, me, section)
+
+    to_sections(send_label, recv_label.at[col], label_send, label_recv)
+    recv_label[col] = send_label[...]
 
     comp_load.wait()
     for s in range(STEPS):
@@ -410,13 +409,11 @@
 
             loop(X // 2, to_ordinates)
 
+    wait_for(recv_label.at[pl.ds(0, SECTIONS - 1)], label_recv)
+
     @pl.when(is_owner)
     def _():
-        @pl.when(owns_other)
-        def _():
-            wait_for(recv_label, label_recv)
-
-        first_own = jnp.broadcast_to(recv_label[0:1, :M], (M, M)) == 0.0
+        first_own = jnp.broadcast_to(recv_label[served_col, 0:1, :M], (M, M)) == 0.0
         left_own[...] = left_operand(jnp.where(first_own, mids[0], mids[1]))
 
         wait_for_slabs(recv_absorb, absorb_recv)
@@ -515,10 +512,6 @@
         both = recv_flow[s].reshape(LANES, LANES).T
         return [both[M * h : M * h + M] for h in range(HALVES)]
 
-    def to_sections(source, target, send_sem, recv_sem):
-        for section in far_sections():
-            remote(source, target, send_sem, recv_sem, me, section)
-
     inflow_first = inflows(0)
     for h in range(HALVES):
         inflow = inflow_first[h]
@@ -534,8 +527,6 @@
             free[1, h, 2 * i + 1] = result[:, LANES:]
 
         loop(X // 2, middle)
-    for s in range(STEPS):
-        send_early[pl.ds(2 * X + 8 * s, 8)] = jnp.broadcast_to(labels[0, s].astype(F32), (8, LANES))
     to_sections(send_early, recv_early.at[col], early_send, early_recv)
     recv_early[col] = send_early[...]
     for h in range(HALVES):
@@ -551,8 +542,8 @@
             send_late[h, pl.ds(i, 1)] = jnp.sum(solved * comp_ordin[1, h, i], axis=0, keepdims=True)
 
         loop(X, last_density)
-        to_sections(send_late.at[h], recv_late.at[h, col], late_send.at[h], late_recv.at[h])
-        recv_late[h, col] = send_late[h]
+    to_sections(send_late, recv_late.at[col], late_send, late_recv)
+    recv_late[col] = send_late[...]
     q_store = [
         pltpu.make_async_copy(q_out.at[h], out_ref.at[:, pl.ds(LANES * h, LANES)], store_sem.at[h])
         for h in range(HALVES)
@@ -573,8 +564,7 @@
     def add_densities(carry, terms, s):
         def one(c, carry):
             total_a, total_b = carry
-            label = recv_early[c, pl.ds(2 * X + 8 * s, 8)]
-            is_a = jnp.concatenate([label, label], axis=0) == 0.0
+            is_a = jnp.broadcast_to(recv_label[c, s : s + 1], (X, LANES)) == 0.0
             term = terms(c)
             return total_a + jnp.where(is_a, term, 0.0), total_b + jnp.where(is_a, 0.0, term)
 
@@ -583,22 +573,19 @@
     none = jnp.zeros((X, LANES), F32)
     early = [add_densities((none, none), lambda c, h=h: recv_early[c, pl.ds(X * h, X)], 0) for h in range(HALVES)]
     for h in range(HALVES):
-        wait_for(recv_late.at[h, pl.ds(0, SECTIONS - 1)], late_recv.at[h])
-        total_a, total_b = add_densities(early[h], lambda c, h=h: recv_late[h, c], 1)
+        if h == 0:
+            wait_for(recv_late.at[pl.ds(0, SECTIONS - 1)], late_recv)
+        total_a, total_b = add_densities(early[h], lambda c, h=h: recv_late[c, h], 1)
         dens_ref[0, :, pl.ds(LANES * h, LANES)] = total_a
         dens_ref[1, :, pl.ds(LANES * h, LANES)] = total_b
 
-    @pl.when(tells)
-    def _():
-        wait_for(send_label, label_send)
-
+    wait_for(recv_label.at[pl.ds(0, SECTIONS - 1)], label_send)
     wait_for_owners(send_absorb, absorb_send)
     for s in range(STEPS):
         wait_for_owners(send_out.at[s], out_send.at[s])
         wait_for_slabs(send_flow.at[s], flow_send.at[s])
     wait_for(recv_early.at[pl.ds(0, SECTIONS - 1)], early_send)
-    for h in range(HALVES):
-        wait_for(recv_late.at[h, pl.ds(0, SECTIONS - 1)], late_send.at[h])
+    wait_for(recv_late.at[pl.ds(0, SECTIONS - 1)], late_send)
     for copy in q_store:
         copy.wait()
 
@@ -671,11 +658,11 @@
         by_slab,
         by_owner,
         pltpu.VMEM((8, LANES), F32),
-        pltpu.VMEM((8, LANES), F32),
-        pltpu.VMEM((3 * X, LANES), F32),
-        pltpu.VMEM((SECTIONS, 3 * X, LANES), F32),
+        pltpu.VMEM((SECTIONS, 8, LANES), F32),
+        pltpu.VMEM((HALVES * X, LANES), F32),
+        pltpu.VMEM((SECTIONS, HALVES * X, LANES), F32),
         pltpu.VMEM((HALVES, X, LANES), F32),
-        pltpu.VMEM((HALVES, SECTIONS, X, LANES), F32),
+        pltpu.VMEM((SECTIONS, HALVES, X, LANES), F32),
         dma((6,)),
         dma((HALVES,)),
         dma,
@@ -689,8 +676,8 @@
         dma,
         dma,
         dma,
-        dma((HALVES,)),
-        dma((HALVES,)),
+        dma,
+        dma,
         dma((HALVES,)),
     ]
     propagated, density = pl.pallas_call(

time: 31.7 us -> 31 us (0.978)
  Pallas kernels: 31 us -> 30.2 us
    pallas_call x1, Pallas kernels: 30 us -> 29.2 us  [body(): pl.pallas_call(kernel, out_shape=(jax.ShapeDtypeStruct((rows, lines), F32...]
where the time goes in v7:
time: 31 us; the launch traced here: 30.9 us
  Pallas kernels  30.2 us (97%)
  between operations  0.64 us (2%)
    pallas_call x1, Pallas kernels, body(): pl.pallas_call(kernel, out_shape=(jax.ShapeDtypeStruct((rows, lines), F32...  29.2 us
    pallas_call x1, Pallas kernels, body(): pl.pallas_call(store, out_shape=(jax.ShapeDtypeStruct((rows, lines), F32)...  1 us

profile of v7, /device:TPU:1, one launch (start us, length us, event | category | flops | bytes accessed | tf_op | source)
XLA Modules:
  0.0 30.9 jit_solution(12588023938132747621)
XLA Ops:
  0.6 29.2 %contour_steps.1 = (f32[1024,256]{1,0:T(8,128)S(1)}, f32[2,16,256]{2,1,0:T(8,128)S(1)}) custom-call(f32[1024,256]{1,0:T(8,128)} %bitcast.4, bf16[2,1024,256]{2,1,0:T(8,128)(2,1)} %bitcast.5, s32[1,2]{1,0:T(1,128)} %labels_ref.1, f32[2,16,256]{2,1,0:T(8,128)} %absorb_ref.1, f32[64,64]{1,0:T(8,128)} %ordin_ref.1, f32[64,64]{1,0:T(8,128)} %modes_ref.1, ...), custom_call_target="tpu_custom_call" | custom-call | tf_op jit(solution)/shard_map/contour_steps/pallas_call | solution.py:683
  29.9 1.0 %store_results.1 = (f32[1024,256]{1,0:T(8,128)}, f32[2,16,256]{2,1,0:T(8,128)}) custom-call(f32[1024,256]{1,0:T(8,128)S(1)} %get-tuple-element.6.q_ref, f32[2,16,256]{2,1,0:T(8,128)S(1)} %get-tuple-element.7.dens_ref), custom_call_target="tpu_custom_call" | custom-call | tf_op jit(solution)/shard_map/store_results/pallas_call | solution.py:711

commit v8 on v7

--- a/solution.py
+++ b/solution.py
@@ -516,19 +516,23 @@
     for h in range(HALVES):
         inflow = inflow_first[h]
 
+        def first_density(i):
+            solved = free[0, h, i] + unit[0, h, i] * inflow
+            free[0, h, i] = solved
+            send_early[pl.ds(X * h + i, 1)] = jnp.sum(solved * comp_ordin[0, h, i], axis=0, keepdims=True)
+
+        loop(X, first_density)
+    to_sections(send_early, recv_early.at[col], early_send, early_recv)
+    recv_early[col] = send_early[...]
+    for h in range(HALVES):
+
         def middle(i):
-            solved = [free[0, h, 2 * i + j] + unit[0, h, 2 * i + j] * inflow for j in range(2)]
-            for j in range(2):
-                send_early[pl.ds(X * h + 2 * i + j, 1)] = jnp.sum(
-                    solved[j] * comp_ordin[0, h, 2 * i + j], axis=0, keepdims=True
-                )
-            result = product(left_mid[...], jnp.concatenate(solved, axis=1))
+            value = jnp.concatenate([free[0, h, 2 * i], free[0, h, 2 * i + 1]], axis=1)
+            result = product(left_mid[...], value)
             free[1, h, 2 * i] = result[:, :LANES]
             free[1, h, 2 * i + 1] = result[:, LANES:]
 
         loop(X // 2, middle)
-    to_sections(send_early, recv_early.at[col], early_send, early_recv)
-    recv_early[col] = send_early[...]
     for h in range(HALVES):
         sweep(1, h)
 

time: 31 us -> 30.9 us (level)
  no operation moved by 1% of the time
where the time goes in v8:
time: 30.9 us; the launch traced here: 30.8 us
  Pallas kernels  30.2 us (98%)
  between operations  0.64 us (2%)
    pallas_call x1, Pallas kernels, body(): pl.pallas_call(kernel, out_shape=(jax.ShapeDtypeStruct((rows, lines), F32...  29.2 us
    pallas_call x1, Pallas kernels, body(): pl.pallas_call(store, out_shape=(jax.ShapeDtypeStruct((rows, lines), F32)...  1 us

profile of v8, /device:TPU:1, one launch (start us, length us, event | category | flops | bytes accessed | tf_op | source)
XLA Modules:
  0.0 30.8 jit_solution(13461856260466004809)
XLA Ops:
  0.6 29.2 %contour_steps.1 = (f32[1024,256]{1,0:T(8,128)S(1)}, f32[2,16,256]{2,1,0:T(8,128)S(1)}) custom-call(f32[1024,256]{1,0:T(8,128)} %bitcast.4, bf16[2,1024,256]{2,1,0:T(8,128)(2,1)} %bitcast.5, s32[1,2]{1,0:T(1,128)} %labels_ref.1, f32[2,16,256]{2,1,0:T(8,128)} %absorb_ref.1, f32[64,64]{1,0:T(8,128)} %ordin_ref.1, f32[64,64]{1,0:T(8,128)} %modes_ref.1, ...), custom_call_target="tpu_custom_call" | custom-call | tf_op jit(solution)/shard_map/contour_steps/pallas_call | solution.py:687
  29.8 1.0 %store_results.1 = (f32[1024,256]{1,0:T(8,128)}, f32[2,16,256]{2,1,0:T(8,128)}) custom-call(f32[1024,256]{1,0:T(8,128)S(1)} %get-tuple-element.6.q_ref, f32[2,16,256]{2,1,0:T(8,128)S(1)} %get-tuple-element.7.dens_ref), custom_call_target="tpu_custom_call" | custom-call | tf_op jit(solution)/shard_map/store_results/pallas_call | solution.py:715

commit v9 on v8

--- a/solution.py
+++ b/solution.py
@@ -18,7 +18,7 @@
 BLOCKS = 2
 RING_Z, RING_Y, RING_X = 8, 4, 4
 FAR_Z, FAR_Y, FAR_X = (4, 3, 5, 2, 6, 1, 7, 0), (2, 1, 3, 0), (2, 1, 3, 0)
-STORES = 2
+STORES = 1
 
 
 def loop(count, step, carry=None):

time: 30.9 us -> 30.9 us (level)
  no operation moved by 1% of the time
where the time goes in v9:
time: 30.9 us; the launch traced here: 30.8 us
  Pallas kernels  30.2 us (98%)
  between operations  0.64 us (2%)
    pallas_call x1, Pallas kernels, body(): pl.pallas_call(kernel, out_shape=(jax.ShapeDtypeStruct((rows, lines), F32...  29.2 us
    pallas_call x1, Pallas kernels, body(): pl.pallas_call(store, out_shape=(jax.ShapeDtypeStruct((rows, lines), F32)...  1 us

profile of v9, /device:TPU:1, one launch (start us, length us, event | category | flops | bytes accessed | tf_op | source)
XLA Modules:
  0.0 30.8 jit_solution(3230971952114274853)
XLA Ops:
  0.6 29.2 %contour_steps.1 = (f32[1024,256]{1,0:T(8,128)S(1)}, f32[2,16,256]{2,1,0:T(8,128)S(1)}) custom-call(f32[1024,256]{1,0:T(8,128)} %bitcast.4, bf16[2,1024,256]{2,1,0:T(8,128)(2,1)} %bitcast.5, s32[1,2]{1,0:T(1,128)} %labels_ref.1, f32[2,16,256]{2,1,0:T(8,128)} %absorb_ref.1, f32[64,64]{1,0:T(8,128)} %ordin_ref.1, f32[64,64]{1,0:T(8,128)} %modes_ref.1, ...), custom_call_target="tpu_custom_call" | custom-call | tf_op jit(solution)/shard_map/contour_steps/pallas_call | solution.py:687
  29.8 1.0 %store_results.1 = (f32[1024,256]{1,0:T(8,128)}, f32[2,16,256]{2,1,0:T(8,128)}) custom-call(f32[1024,256]{1,0:T(8,128)S(1)} %get-tuple-element.6.q_ref, f32[2,16,256]{2,1,0:T(8,128)S(1)} %get-tuple-element.7.dens_ref), custom_call_target="tpu_custom_call" | custom-call | tf_op jit(solution)/shard_map/store_results/pallas_call | solution.py:715
